TPU v7x, 128 devices: a whole 4x4x4 slice. The times are simulated.
128 devices in a mesh: dp: 2 (over x_lo), ctx: 64 (over y, z, x_hi, core).
Axes of the slice: x: 4 (x_hi: 2, x_lo: 2; x = x_hi * 2 + x_lo), y: 4, z: 4, core: 2. Of those that a mesh axis runs over, the one named last changes fastest.
Arguments:
- saved_input: bfloat16 [2, 32768, 512], P('dp', 'ctx'), may hold values from -6 to 6
- output_grad: bfloat16 [2, 32768, 512], P('dp', 'ctx'), may hold values from -0.0625 to 0.0625
- filter_taps: bfloat16 [32768, 512], P('ctx'), may hold values from -6 to 6
Outputs:
- input_grad: bfloat16 [2, 32768, 512], P('dp', 'ctx')
- filter_grad: float32 [32768, 512], P('ctx', 'dp')
All inputs are finite; a program needn't handle non-finite values.
Results may differ from a plain program's by a relative error of at most 0.001.
Values may be sent and summed in bfloat16 or wider, within the bound.
No kernel may reach another device: no remote copies, remote signals or barrier semaphores. Data moves between devices by JAX's collectives and lax.ppermute only.
A program may use at most 128 MiB of HBM per device.

v0:
```python
import math

import jax
import jax.numpy as jnp
from jax import lax
from jax.sharding import PartitionSpec as P

highest = lax.Precision.HIGHEST


def angles(row_ids, col_ids, period):
    product = row_ids[:, None] * col_ids[None, :] % period
    return product.astype(jnp.float32) * (2.0 * math.pi / period)


def first_section(signal, offset, fft_length):
    row_count = signal.shape[0]
    col_count = signal.shape[1]
    source = jnp.arange(row_count, dtype=jnp.int32)
    target = jnp.arange(2 * row_count, dtype=jnp.int32)
    phases = angles(source, target, 2 * row_count)
    values = signal.astype(jnp.float32)
    real_part = jnp.einsum("nk,nsc->ksc", jnp.cos(phases), values, precision=highest)
    imag_part = -jnp.einsum("nk,nsc->ksc", jnp.sin(phases), values, precision=highest)
    offsets = offset + jnp.arange(col_count, dtype=jnp.int32)
    turn_angle = angles(target, offsets, fft_length)[:, :, None]
    cosine = jnp.cos(turn_angle)
    sine_part = jnp.sin(turn_angle)
    return (real_part * cosine + imag_part * sine_part, imag_part * cosine - real_part * sine_part)


def middle_section(real_part, imag_part, exponent_sign):
    length = real_part.shape[1]
    indices = jnp.arange(length, dtype=jnp.int32)
    phases = angles(indices, indices, length)
    cosine = jnp.cos(phases)
    sine_part = jnp.sin(phases)

    def contract(matrix, operand):
        flat = operand.reshape(operand.shape[0], length, -1)
        result = jnp.einsum("nk,anm->akm", matrix, flat, precision=highest)
        return result.reshape(operand.shape)

    if exponent_sign < 0:
        return (
            contract(cosine, real_part) + contract(sine_part, imag_part),
            contract(cosine, imag_part) - contract(sine_part, real_part),
        )
    return (
        contract(cosine, real_part) - contract(sine_part, imag_part),
        contract(cosine, imag_part) + contract(sine_part, real_part),
    )


def inverse_turn(real_part, imag_part, offset, fft_length):
    row_count = real_part.shape[0]
    length = real_part.shape[1]
    row_ids = offset + jnp.arange(row_count, dtype=jnp.int32)
    phases = angles(row_ids, jnp.arange(length, dtype=jnp.int32), fft_length)
    shape_out = (row_count, length) + (1,) * (real_part.ndim - 2)
    cosine = jnp.cos(phases).reshape(shape_out)
    sine_part = jnp.sin(phases).reshape(shape_out)
    return (real_part * cosine - imag_part * sine_part, imag_part * cosine + real_part * sine_part)


def last_section(real_part, imag_part, fft_length):
    row_count = real_part.shape[0]
    half_rows = row_count // 2
    phases = angles(
        jnp.arange(row_count, dtype=jnp.int32), jnp.arange(half_rows, dtype=jnp.int32), row_count
    )
    cosine = jnp.cos(phases)
    sine_part = jnp.sin(phases)
    factor = 1.0 / fft_length

    def contract(matrix, operand):
        flat = operand.reshape(row_count, -1)
        result = jnp.einsum("kn,km->nm", matrix, flat, precision=highest)
        return result.reshape((half_rows,) + operand.shape[1:])

    out_real = (contract(cosine, real_part) - contract(sine_part, imag_part)) * factor
    return out_real


def products(freq_real, freq_imag):
    sig_re = freq_real[:, :, 0]
    sig_im = freq_imag[:, :, 0]
    grad_re = freq_real[:, :, 1]
    grad_im = freq_imag[:, :, 1]
    filt_re = freq_real[:, :, 2]
    filt_im = freq_imag[:, :, 2]
    input_re = grad_re * filt_re + grad_im * filt_im
    input_im = grad_im * filt_re - grad_re * filt_im
    filter_re = grad_re * sig_re + grad_im * sig_im
    filter_im = grad_im * sig_re - grad_re * sig_im
    return (
        jnp.concatenate([input_re, filter_re], axis=-1),
        jnp.concatenate([input_im, filter_im], axis=-1),
    )


def split_outputs(time_parts, chan_count):
    return (time_parts[..., :chan_count], time_parts[..., chan_count:])


def shards(saved_input, output_grad, filter_taps):
    ctx_count = lax.axis_size("ctx")
    ctx_index = lax.axis_index("ctx")
    local_len = saved_input.shape[1]
    chan_count = saved_input.shape[2]
    fft_length = 2 * ctx_count * local_len
    filter_rows = filter_taps[None]
    pieces = (
        lax.all_to_all(saved_input, "ctx", split_axis=1, concat_axis=0, tiled=True),
        lax.all_to_all(output_grad, "ctx", split_axis=1, concat_axis=0, tiled=True),
        lax.all_to_all(filter_rows, "ctx", split_axis=1, concat_axis=0, tiled=True),
    )
    column_step = local_len // ctx_count
    turned = [first_section(entry, ctx_index * column_step, fft_length) for entry in pieces]
    stacked = jnp.stack(
        [turned[0][0], turned[0][1], turned[1][0], turned[1][1], turned[2][0], turned[2][1]], axis=2
    )
    received = lax.all_to_all(stacked, "ctx", split_axis=0, concat_axis=1, tiled=True)
    freq_real, freq_imag = middle_section(received[:, :, 0::2], received[:, :, 1::2], -1)
    spec_real, spec_imag = products(freq_real, freq_imag)
    back_real, back_imag = middle_section(spec_real, spec_imag, 1)
    back_real, back_imag = inverse_turn(back_real, back_imag, 2 * ctx_index, fft_length)
    joined = jnp.stack([back_real, back_imag], axis=2)
    received = lax.all_to_all(joined, "ctx", split_axis=1, concat_axis=0, tiled=True)
    time_parts = last_section(received[:, :, 0], received[:, :, 1], fft_length)
    input_time, filter_time = split_outputs(time_parts, chan_count)
    input_grad = lax.all_to_all(
        input_time.astype(jnp.bfloat16), "ctx", split_axis=0, concat_axis=1, tiled=True
    )
    filter_part = lax.all_to_all(filter_time, "ctx", split_axis=0, concat_axis=1, tiled=True)
    filter_grad = lax.psum_scatter(filter_part[0], "dp", scatter_dimension=1, tiled=True)
    return (input_grad, filter_grad)


def solution(mesh):
    placed = (P("dp", "ctx", None), P("dp", "ctx", None), P("ctx", None))
    return jax.shard_map(
        shards,
        mesh=mesh,
        in_specs=placed,
        out_specs=(P("dp", "ctx", None), P("ctx", "dp")),
        check_vma=False,
    )
```

profile of v0, /device:TPU:1, one launch (start us, length us, event | category | flops | bytes accessed | tf_op | source)
XLA Modules:
  0.0 689.4 jit_solution(15411724045815998065)
XLA Ops:
  14.6 12.5 %all-to-all-start = ((bf16[64,2,2048]{2,1,0:T(2,128)(2,1)}), bf16[64,2,2048]{2,1,0:T(2,128)(2,1)S(1)}, u32[]{:S(2)}, u32[]{:S(2)}) async-start(bf16[64,2,2048]{2,1,0:T(2,128)(2,1)} %reshape.174), calls=%async_computation | async-start | bytes 1048576 | tf_op jit(solution)/shard_map/all_to_all | solution.py:114
  32.8 8.6 %all-to-all-done = bf16[64,2,2048]{2,1,0:T(2,128)(2,1)S(1)} async-done(((bf16[64,2,2048]{2,1,0:T(2,128)(2,1)}), bf16[64,2,2048]{2,1,0:T(2,128)(2,1)S(1)}, u32[]{:S(2)}, u32[]{:S(2)}) %all-to-all-start) | async-done | bytes 524320 | tf_op jit(solution)/shard_map/all_to_all | solution.py:114
  41.4 4.8 all-to-all-start.1
  52.7 7.8 %all-to-all-done.1 = bf16[64,2,2048]{2,1,0:T(2,128)(2,1)S(1)} async-done(((bf16[64,2,2048]{2,1,0:T(2,128)(2,1)}), bf16[64,2,2048]{2,1,0:T(2,128)(2,1)S(1)}, u32[]{:S(2)}, u32[]{:S(2)}) %all-to-all-start.1) | async-done | bytes 524320 | tf_op jit(solution)/shard_map/all_to_all | solution.py:115
  60.5 5.3 all-to-all-start.2
  70.2 10.0 %all-to-all-done.2 = bf16[64,2,2048]{2,1,0:T(2,128)(2,1)} async-done(((bf16[64,2,2048]{2,1,0:T(2,128)(2,1)}), bf16[64,2,2048]{2,1,0:T(2,128)(2,1)}, u32[]{:S(2)}, u32[]{:S(2)}) %all-to-all-start.2) | async-done | bytes 524320 | tf_op jit(solution)/shard_map/all_to_all | solution.py:116
  80.1 4.6 reshape.179
  100.9 16.8 %copy.65 = f32[128,8,6,512]{3,1,2,0:T(8,128)} copy(f32[128,8,6,512]{3,0,1,2:T(8,128)} %bitcast_dynamic-update-slice_fusion) | data formatting | bytes 25165824 | tf_op jit(solution)/shard_map/stack | solution.py:120
  117.7 5.6 all-to-all-start.3
  123.5 154.8 %all-to-all-done.3 = f32[128,8,6,512]{3,1,2,0:T(8,128)} async-done(((f32[128,8,6,512]{3,1,2,0:T(8,128)}), f32[128,8,6,512]{3,1,2,0:T(8,128)}, u32[]{:S(2)}, u32[]{:S(2)}) %all-to-all-start.3) | async-done | bytes 12582944 | tf_op jit(solution)/shard_map/all_to_all | solution.py:123
  278.3 11.4 %copy.119 = f32[2,64,8,6,512]{4,2,1,3,0:T(8,128)} copy(f32[2,64,8,6,512]{4,2,3,0,1:T(8,128)} %bitcast.11) | data formatting | bytes 25165824 | tf_op jit(solution)/shard_map/all_to_all | solution.py:123
  289.7 10.6 %fusion.163 = (f32[2,512,3,512]{3,1,2,0:T(8,128)}, f32[2,512,3,512]{3,1,2,0:T(8,128)}) fusion(f32[2,512,6,512]{3,1,2,0:T(8,128)} %bitcast.188), kind=kLoop, calls=%fused_computation.192 | loop fusion | bytes 25165824 | tf_op jit(solution)/shard_map/slice | solution.py:124
  300.2 6.6 copy.68
  306.8 18.6 %fusion.21 = f32[2,1536,512]{2,1,0:T(8,128)} fusion(f32[2,512,1536]{1,2,0:T(8,128)} %bitcast.182), kind=kOutput, calls=%fused_computation.49 | convolution fusion | flops 9667346432 | bytes 12582912 | tf_op jit(solution)/shard_map/nk,anm->akm/dot_general | solution.py:41
  325.4 6.7 copy.67
  332.1 19.2 %fusion.23 = f32[2,1536,512]{2,1,0:T(8,128)} fusion(f32[2,512,1536]{1,2,0:T(8,128)} %bitcast.186), kind=kOutput, calls=%fused_computation.51 | convolution fusion | flops 9667346432 | bytes 12582912 | tf_op jit(solution)/shard_map/nk,anm->akm/dot_general | solution.py:41
  351.4 14.5 %convolution_subtract_fusion = f32[2,1536,512]{2,1,0:T(8,128)S(1)} fusion(f32[2,1536,512]{2,1,0:T(8,128)S(1)} %bitcast.194, f32[2,512,1536]{1,2,0:T(8,128)S(1)} %bitcast.187), kind=kOutput, calls=%fused_computation.3 | convolution fusion | flops 9668919296 | bytes 18874368 | tf_op jit(solution)/shard_map/nk,anm->akm/dot_general | solution.py:41
  365.9 21.4 %convolution_add_fusion = f32[2,1536,512]{2,1,0:T(8,128)S(1)} fusion(f32[2,1536,512]{2,1,0:T(8,128)} %fusion.23, f32[2,512,1536]{1,2,0:T(8,128)S(1)} %bitcast.185), kind=kOutput, calls=%fused_computation.4 | convolution fusion | flops 9668919296 | bytes 18874368 | tf_op jit(solution)/shard_map/nk,anm->akm/dot_general | solution.py:41
  387.3 5.3 add_bitcast_fusion.2
  392.6 13.6 %fusion.4 = f32[2,1024,512]{2,1,0:T(8,128)S(1)} fusion(f32[2,512,512]{1,2,0:T(8,128)} %get-tuple-element.4, f32[2,512,512]{1,2,0:T(8,128)} %get-tuple-element.3), kind=kOutput, calls=%fused_computation.13 | convolution fusion | flops 6447169536 | bytes 8388608 | tf_op jit(solution)/shard_map/nk,anm->akm/dot_general | solution.py:41
  406.2 11.6 %fusion.5 = f32[2,1024,512]{2,1,0:T(8,128)S(1)} fusion(f32[2,512,512]{1,2,0:T(8,128)S(1)} %copy-done.6, f32[2,512,512]{1,2,0:T(8,128)S(1)} %copy-done.5), kind=kOutput, calls=%fused_computation.14 | convolution fusion | flops 6447169536 | bytes 8388608 | tf_op jit(solution)/shard_map/nk,anm->akm/dot_general | solution.py:41
  417.9 11.3 %fusion.8 = f32[2,1024,512]{2,1,0:T(8,128)S(1)} fusion(f32[2,1024,512]{2,1,0:T(8,128)S(1)} %fusion.5, f32[2,512,512]{1,2,0:T(8,128)S(1)} %copy-done.2, f32[2,512,512]{1,2,0:T(8,128)S(1)} %copy-done.1), kind=kOutput, calls=%fused_computation.17 | convolution fusion | flops 6448218112 | bytes 12582912 | tf_op jit(solution)/shard_map/nk,anm->akm/dot_general | solution.py:41
  429.2 12.1 %subtract_bitcast_fusion = (f32[2,512,1,1024]{1,3,0,2:T(8,128)S(1)}, f32[2,512,1,1024]{1,3,0,2:T(8,128)S(1)}) fusion(f32[2,1024,512]{2,1,0:T(8,128)S(1)} %fusion.8, f32[2,512]{1,0:T(2,128)S(1)} %get-tuple-element.13, f32[2,512]{1,0:T(2,128)S(1)} %get-tuple-element.12, f32[2,1024,512]{2,1,0:T(8,128)S(1)} %fusion.4, f32[2,512,512]{1,2,0:T(8,128)S(1)} %copy-done.2, ...), kind=kOutput, calls=%fused_computation.12 | convolution fusion | flops 6454509568 | bytes 20979712 | tf_op jit(solution)/shard_map/nk,anm->akm/dot_general | solution.py:41
  445.8 13.4 %copy.75 = f32[2,512,2,1024]{3,0,2,1:T(2,128)} copy(f32[2,512,2,1024]{1,3,0,2:T(8,128)} %pad_maximum_fusion) | data formatting | bytes 16777216 | tf_op jit(solution)/shard_map/stack | solution.py:128
  459.2 131.8 %all_to_all.93 = f32[2,512,2,1024]{3,0,2,1:T(2,128)S(1)} all-to-all(f32[2,512,2,1024]{3,0,2,1:T(2,128)} %copy.75), channel_id=1, replica_groups=mesh['dp'=2,'ctx'=64] {'ctx'}, dimensions={1} | all-to-all | bytes 16777216 | tf_op jit(solution)/shard_map/all_to_all | solution.py:129
  591.0 4.9 copy.120
  601.6 5.4 copy.83
  607.0 6.8 fusion
  613.8 5.7 copy.82
  619.5 6.9 subtract_multiply_fusion
  628.4 27.1 %all_to_all.94 = f32[64,8,512]{2,1,0:T(8,128)} all-to-all(f32[64,8,512]{2,1,0:T(8,128)S(1)} %copy.81), channel_id=1, replica_groups=mesh['dp'=2,'ctx'=64] {'ctx'}, dimensions={0} | all-to-all | bytes 2097152 | tf_op jit(solution)/shard_map/all_to_all | solution.py:135
  657.2 24.2 %all_to_all.95 = bf16[64,8,512]{2,1,0:T(8,128)(2,1)S(1)} all-to-all(bf16[64,8,512]{2,1,0:T(8,128)(2,1)S(1)} %copy.80), channel_id=1, replica_groups=mesh['dp'=2,'ctx'=64] {'ctx'}, dimensions={0} | all-to-all | bytes 1048576 | tf_op jit(solution)/shard_map/all_to_all | solution.py:132
  (67 shorter events, 54.8 us)
Async XLA Ops:
  7.2 19.9 %copy-start.7 = (bf16[1,512,512]{2,1,0:T(8,128)(2,1)S(1)}, bf16[1,512,512]{2,1,0:T(8,128)(2,1)}, u32[]{:S(2)}) copy-start(bf16[1,512,512]{2,1,0:T(8,128)(2,1)} %param.4) | copy-start | bytes 1572868
  9.7 36.5 %copy-start.8 = (bf16[512,512]{1,0:T(8,128)(2,1)S(1)}, bf16[512,512]{1,0:T(8,128)(2,1)}, u32[]{:S(2)}) copy-start(bf16[512,512]{1,0:T(8,128)(2,1)} %param.5) | copy-start | bytes 1572868
  14.6 26.8 %all-to-all-start = ((bf16[64,2,2048]{2,1,0:T(2,128)(2,1)}), bf16[64,2,2048]{2,1,0:T(2,128)(2,1)S(1)}, u32[]{:S(2)}, u32[]{:S(2)}) async-start(bf16[64,2,2048]{2,1,0:T(2,128)(2,1)} %reshape.174), calls=%async_computation | async-start | bytes 1048576 | tf_op jit(solution)/shard_map/all_to_all | solution.py:114
  41.4 19.1 %all-to-all-start.1 = ((bf16[64,2,2048]{2,1,0:T(2,128)(2,1)}), bf16[64,2,2048]{2,1,0:T(2,128)(2,1)S(1)}, u32[]{:S(2)}, u32[]{:S(2)}) async-start(bf16[64,2,2048]{2,1,0:T(2,128)(2,1)} %reshape.176), calls=%async_computation.1 | async-start | bytes 1048576 | tf_op jit(solution)/shard_map/all_to_all | solution.py:115
  60.5 19.7 %all-to-all-start.2 = ((bf16[64,2,2048]{2,1,0:T(2,128)(2,1)}), bf16[64,2,2048]{2,1,0:T(2,128)(2,1)}, u32[]{:S(2)}, u32[]{:S(2)}) async-start(bf16[64,2,2048]{2,1,0:T(2,128)(2,1)} %reshape.178), calls=%async_computation.2 | async-start | bytes 1048576 | tf_op jit(solution)/shard_map/all_to_all | solution.py:116
  84.8 2.7 copy-start.3
  117.7 160.6 %all-to-all-start.3 = ((f32[128,8,6,512]{3,1,2,0:T(8,128)}), f32[128,8,6,512]{3,1,2,0:T(8,128)}, u32[]{:S(2)}, u32[]{:S(2)}) async-start(f32[128,8,6,512]{3,1,2,0:T(8,128)} %copy.65), calls=%async_computation.3 | async-start | bytes 25165824 | tf_op jit(solution)/shard_map/all_to_all | solution.py:123
  123.3 558.0 %reduce-scatter.2.cloned.1.call-start = ((), (), s32[]{:S(2)}) async-start(), calls=%async_computation.8 | async-start | bytes 1572864 | tf_op jit(solution)/shard_map/reduce_scatter | solution.py:136
  325.4 25.9 %slice-start.2 = ((s8[6291456]{0:T(1024)(128)(4,1)}), s8[2097152]{0:T(1024)(128)(4,1)S(1)}, s32[]{:S(2)}) async-start(s8[6291456]{0:T(1024)(128)(4,1)} %bitcast.193), calls=%async_computation.11 | async-start | bytes 4194304
  332.1 19.2 %copy-start = (f32[2,512,3,512]{1,3,2,0:T(8,128)S(1)}, f32[2,512,3,512]{1,3,2,0:T(8,128)}, u32[]{:S(2)}) copy-start(f32[2,512,3,512]{1,3,2,0:T(8,128)} %copy.67) | copy-start | bytes 18874372
  332.1 19.2 %slice-start.3 = ((s8[6291456]{0:T(1024)(128)(4,1)}), s8[4194304]{0:T(1024)(128)(4,1)S(1)}, s32[]{:S(2)}) async-start(s8[6291456]{0:T(1024)(128)(4,1)} %bitcast.193), calls=%async_computation.12 | async-start | bytes 8388608
  332.1 33.7 %slice-start = ((s8[6291456]{0:T(1024)(128)(4,1)}), s8[4194304]{0:T(1024)(128)(4,1)S(1)}, s32[]{:S(2)}) async-start(s8[6291456]{0:T(1024)(128)(4,1)} %bitcast.183), calls=%async_computation.9 | async-start | bytes 8388608
  351.3 14.5 %slice-start.1 = ((s8[6291456]{0:T(1024)(128)(4,1)}), s8[2097152]{0:T(1024)(128)(4,1)S(1)}, s32[]{:S(2)}) async-start(s8[6291456]{0:T(1024)(128)(4,1)} %bitcast.183), calls=%async_computation.10 | async-start | bytes 4194304
  392.6 13.6 %copy-start.5 = (f32[2,512,512]{1,2,0:T(8,128)S(1)}, f32[2,512,512]{1,2,0:T(8,128)}, u32[]{:S(2)}) copy-start(f32[2,512,512]{1,2,0:T(8,128)} %get-tuple-element.3) | copy-start | bytes 6291460
  392.6 13.6 %copy-start.6 = (f32[2,512,512]{1,2,0:T(8,128)S(1)}, f32[2,512,512]{1,2,0:T(8,128)}, u32[]{:S(2)}) copy-start(f32[2,512,512]{1,2,0:T(8,128)} %get-tuple-element.4) | copy-start | bytes 6291460
  406.2 11.7 %copy-start.1 = (f32[2,512,512]{1,2,0:T(8,128)S(1)}, f32[2,512,512]{1,2,0:T(8,128)}, u32[]{:S(2)}) copy-start(f32[2,512,512]{1,2,0:T(8,128)} %get-tuple-element.2) | copy-start | bytes 6291460
  406.2 11.7 %copy-start.2 = (f32[2,512,512]{1,2,0:T(8,128)S(1)}, f32[2,512,512]{1,2,0:T(8,128)}, u32[]{:S(2)}) copy-start(f32[2,512,512]{1,2,0:T(8,128)} %get-tuple-element.5) | copy-start | bytes 6291460
  626.4 1.3 copy-start.4
Sparse Core Ops, SparseCore 0:
  655.7 20.2 reduce-scatter.1
where the time goes:
time: 699 us; the launch traced here: 689 us
  blocking collectives  183 us (26%)
  waiting for transfers between devices  181 us (26%)
  matrix products  149 us (21%)
  local copies, waits for them, and re-layouts  106 us (15%)
  starting transfers between devices  28.3 us (4%)
  other arithmetic  26.9 us (4%)
  between operations  14.9 us (2%)
    all_to_all x1, waiting for transfers between devices, shards(): lax.all_to_all(stacked, 'ctx', split_axis=0, concat_axis=1, tiled=True)  155 us
    all_to_all x1, blocking collectives, shards(): lax.all_to_all(joined, 'ctx', split_axis=1, concat_axis=0, tiled=True)  132 us
    dot_general x8, matrix products, contract(): result = jnp.einsum('nk,anm->akm', matrix, flat, precision=highest)  122 us
    all_to_all x1, blocking collectives, shards(): lax.all_to_all(filter_time, 'ctx', split_axis=0, concat_axis=1, tiled=True)  27.1 us
    all_to_all x1, blocking collectives, shards(): lax.all_to_all(input_time.astype(jnp.bfloat16), 'ctx', split_axis=0, conc...  24.2 us
    slice x2, local copies, waits for them, and re-layouts, shards(): received[:, :, 1::2]  17.2 us
    another operation x1, local copies, waits for them, and re-layouts, shards(): jnp.stack([turned[0][0], turned[0][1], turned[1][0], turned[1][1], turned...  16.8 us
    unnamed x39, local copies, waits for them, and re-layouts  15.9 us
  transfers between devices with their start and end apart: 5, of which 4 were waited for; matrix products, arithmetic and copies ran while one was open for 3% of the time, Pallas kernels for 0%

commit v1 on v0

v1 whole, which is shorter than its diff:
```python
import functools
import math

import jax
import jax.numpy as jnp
import ml_dtypes
import numpy as np
from jax import lax
from jax.experimental import pallas as pl
from jax.experimental.pallas import tpu as pltpu
from jax.sharding import PartitionSpec as P

LANES = 128
BF16 = jnp.bfloat16
F32 = jnp.float32
OWN = 4
BATCH = 2


def two_parts(matrix):
    high = matrix.astype(ml_dtypes.bfloat16)
    low = (matrix - high.astype(np.float64)).astype(ml_dtypes.bfloat16)
    return high, low


def turn(numerator, period):
    phase = (numerator % period) * (2.0 * math.pi / period)
    return np.cos(phase), np.sin(phase)


@functools.cache
def tables(seq):
    rows = seq // LANES
    k1 = np.arange(rows, dtype=np.int64)[:, None]
    a = np.arange(rows, dtype=np.int64)[None, :]
    r = np.arange(LANES, dtype=np.int64)
    cos_a, sin_a = turn((4 * k1 + 1) * a, 4 * rows)
    first = np.concatenate([cos_a, -sin_a], axis=0)
    last = np.concatenate([cos_a.T, -sin_a.T], axis=1) / seq
    cos_t, sin_t = turn((4 * k1 + 1) * r[None, :], 4 * seq)
    cos_r, sin_r = turn(r[:, None] * r[None, :], LANES)
    forth = np.block([[cos_r, -sin_r], [sin_r, cos_r]])
    back = np.block([[cos_r, sin_r], [-sin_r, cos_r]])
    return (
        np.concatenate(two_parts(first), axis=0),
        np.concatenate(two_parts(last), axis=0),
        np.concatenate(two_parts(forth), axis=0),
        np.concatenate(two_parts(back), axis=0),
        np.concatenate([cos_t, sin_t], axis=0).astype(np.float32),
    )


def dot(left, right):
    return jnp.dot(left, right, preferred_element_type=F32)


def split(value):
    high = value.astype(BF16)
    return high, (value - high.astype(F32)).astype(BF16)


def pack_kernel(peers, dp_index, u_ref, g_ref, h_ref, out_ref, held):
    blocks = u_ref.shape[0] // LANES
    group = peers // 2

    def place(ref, block, row):
        flipped = ref[block * LANES : (block + 1) * LANES, :].astype(F32).T
        for c in range(OWN):
            held[pl.ds(row + c, peers, stride=40), :] = flipped[c * peers : (c + 1) * peers, :]

    for q in range(blocks):
        place(u_ref, q, OWN * q)
        place(g_ref, q, 16 + OWN * q)
    for q in range(2):
        place(h_ref, q, 32 + OWN * q)
    out_ref[...] = held[...].reshape(peers, 40, LANES).astype(BF16)


def unpack_kernel(peers, in_ref, input_ref, filter_ref, held):
    blocks = input_ref.shape[0] // LANES
    held[...] = in_ref[...].astype(F32).reshape(peers * 32, LANES)
    for q in range(blocks):
        rows = slice(q * LANES, (q + 1) * LANES)
        for c in range(OWN):
            piece = held[pl.ds(OWN * q + c, peers, stride=32), :]
            input_ref[rows, c * peers : (c + 1) * peers] = piece.T.astype(BF16)
        for c in range(OWN // 2):
            high = held[pl.ds(16 + 2 * q + c, peers, stride=32), :]
            low = held[pl.ds(24 + 2 * q + c, peers, stride=32), :]
            filter_ref[rows, c * peers : (c + 1) * peers] = (high + low).T


def convolve_kernel(group, in_ref, first_ref, last_ref, forth_ref, back_ref, turn_ref, out_ref, u_held, g_held, h_held, in_grad, taps_grad):
    rows = group * OWN
    for b in range(BATCH):
        got = in_ref[b * group : (b + 1) * group].astype(F32)
        u_held[b] = got[:, 0:16].reshape(group * 16, LANES)
        g_held[b] = got[:, 16:32].reshape(group * 16, LANES)
    taps = [in_ref[b * group : (b + 1) * group].astype(F32)[:, 32:40] for b in range(BATCH)]
    h_held[0] = jnp.concatenate(taps, axis=1).reshape(group * 16, LANES)
    turn_cos = turn_ref[0:rows, :]
    turn_sin = turn_ref[rows : 2 * rows, :]

    def forward(held, b, channels):
        pair = jnp.concatenate(
            [held[b, pl.ds(c, rows, stride=OWN), :].astype(BF16) for c in channels], axis=1
        )
        both = dot(first_ref[0 : 2 * rows, :], pair) + dot(first_ref[2 * rows : 4 * rows, :], pair)
        spectra = []
        for i in range(len(channels)):
            lanes = slice(i * LANES, (i + 1) * LANES)
            real, imag = both[0:rows, lanes], both[rows : 2 * rows, lanes]
            turned = jnp.concatenate(
                [real * turn_cos + imag * turn_sin, imag * turn_cos - real * turn_sin], axis=1
            )
            spectra.append(across(turned, forth_ref))
        return spectra

    def across(value, matrix_ref):
        high, low = split(value)
        width = 2 * LANES
        return (
            dot(high, matrix_ref[0:width, :])
            + dot(low, matrix_ref[0:width, :])
            + dot(high, matrix_ref[width : 2 * width, :])
        )

    def parts(spectrum):
        return spectrum[:, :LANES], spectrum[:, LANES:]

    def correlate(left, right):
        left_re, left_im = parts(left)
        right_re, right_im = parts(right)
        return jnp.concatenate(
            [left_re * right_re + left_im * right_im, left_im * right_re - left_re * right_im], axis=1
        )

    def backward(products):
        reals, imags = [], []
        for product in products:
            real, imag = parts(across(product, back_ref))
            reals.append(real * turn_cos - imag * turn_sin)
            imags.append(imag * turn_cos + real * turn_sin)
        stacked = jnp.concatenate([jnp.concatenate(reals, axis=1), jnp.concatenate(imags, axis=1)], axis=0)
        high, low = split(stacked)
        return dot(last_ref[0:rows, :], high) + dot(last_ref[0:rows, :], low) + dot(last_ref[rows : 2 * rows, :], high)

    for half in range(2):
        channels = (2 * half, 2 * half + 1)
        taps_spec = forward(h_held, 0, channels)
        grad_spec = [forward(g_held, b, channels) for b in range(BATCH)]
        for b in range(BATCH):
            result = backward([correlate(grad_spec[b][i], taps_spec[i]) for i in range(2)])
            for i in range(2):
                in_grad[b, pl.ds(channels[i], rows, stride=OWN), :] = result[:, i * LANES : (i + 1) * LANES]
        signal_spec = [forward(u_held, b, channels) for b in range(BATCH)]
        result = backward(
            [correlate(grad_spec[0][i], signal_spec[0][i]) + correlate(grad_spec[1][i], signal_spec[1][i]) for i in range(2)]
        )
        for i in range(2):
            taps_grad[half, pl.ds(i, rows, stride=2), :] = result[:, i * LANES : (i + 1) * LANES]
    for d in range(2):
        taps_out = taps_grad[d].reshape(group, 8, LANES)
        high = taps_out.astype(BF16).astype(F32)
        out_ref[d * group : (d + 1) * group] = jnp.concatenate(
            [in_grad[d].reshape(group, 16, LANES), high, taps_out - high], axis=1
        ).astype(BF16)


def shards(saved_input, output_grad, filter_taps):
    group = lax.axis_size("ctx")
    peers = 2 * group
    local_len, chan_count = filter_taps.shape
    seq = group * local_len
    rows = seq // LANES
    constants = [jnp.asarray(table) for table in tables(seq)]
    params = pltpu.CompilerParams(vmem_limit_bytes=48 * 1024 * 1024)
    own_taps = lax.dynamic_slice_in_dim(filter_taps, lax.axis_index("dp") * (local_len // 2), local_len // 2, 0)
    packed = pl.pallas_call(
        functools.partial(pack_kernel, peers, None),
        out_shape=jax.ShapeDtypeStruct((peers, 40, LANES), BF16),
        scratch_shapes=[pltpu.VMEM((peers * 40, LANES), F32)],
        compiler_params=params,
        name="pack",
    )(saved_input[0], output_grad[0], own_taps)
    received = lax.all_to_all(packed, ("dp", "ctx"), split_axis=0, concat_axis=0, tiled=True)
    results = pl.pallas_call(
        functools.partial(convolve_kernel, group),
        out_shape=jax.ShapeDtypeStruct((peers, 32, LANES), BF16),
        scratch_shapes=[
            pltpu.VMEM((BATCH, group * 16, LANES), F32),
            pltpu.VMEM((BATCH, group * 16, LANES), F32),
            pltpu.VMEM((1, group * 16, LANES), F32),
            pltpu.VMEM((BATCH, group * 16, LANES), F32),
            pltpu.VMEM((BATCH, group * 8, LANES), F32),
        ],
        compiler_params=params,
        name="convolve",
    )(received, *constants)
    returned = lax.all_to_all(results, ("dp", "ctx"), split_axis=0, concat_axis=0, tiled=True)
    input_grad, filter_grad = pl.pallas_call(
        functools.partial(unpack_kernel, peers),
        out_shape=(
            jax.ShapeDtypeStruct((local_len, chan_count), BF16),
            jax.ShapeDtypeStruct((local_len, chan_count // 2), F32),
        ),
        scratch_shapes=[pltpu.VMEM((peers * 32, LANES), F32)],
        compiler_params=params,
        name="unpack",
    )(returned)
    return input_grad[None], filter_grad


def solution(mesh):
    placed = (P("dp", "ctx", None), P("dp", "ctx", None), P("ctx", None))
    return jax.shard_map(
        shards,
        mesh=mesh,
        in_specs=placed,
        out_specs=(P("dp", "ctx", None), P("ctx", "dp")),
        check_vma=False,
    )
```

time: 699 us -> 72.5 us (0.10); the launches traced: 689 us -> 72.2 us
  waiting for transfers between devices: 181 us -> 0 us
  matrix products: 149 us -> 0 us
  blocking collectives: 183 us -> 56.9 us
  local copies, waits for them, and re-layouts: 106 us -> 3.17 us
  starting transfers between devices: 28.3 us -> 0 us
  other arithmetic: 26.9 us -> 0 us
  between operations: 14.9 us -> 0.73 us
  Pallas kernels: 0 us -> 11.4 us
    all_to_all x4 -> x0, waiting for transfers between devices: 181 us -> none  [the longest x1 155 us: shards(): lax.all_to_all(stacked, 'ctx', split_axis=0, concat_axis=1, tiled=True)]
    dot_general x16 -> x0, matrix products: 149 us -> none  [the longest x8 122 us: contract(): result = jnp.einsum('nk,anm->akm', matrix, flat, precision=highest)]
    all_to_all x3 -> x2, blocking collectives: 183 us -> 56.9 us  [the longest x1 33.3 us: shards(): lax.all_to_all(packed, ('dp', 'ctx'), split_axis=0, concat_axis=0, tiled=...]
    another operation x4 -> x0, local copies, waits for them, and re-layouts: 41.2 us -> none  [the longest x1 16.8 us: shards(): jnp.stack([turned[0][0], turned[0][1], turned[1][0], turned[1][1], turned...]
    slice x8 -> x0, local copies, waits for them, and re-layouts: 30.3 us -> none  [the longest x2 17.2 us: shards(): received[:, :, 1::2]]
    all_to_all x4 -> x0, starting transfers between devices: 28.3 us -> none  [the longest x1 12.5 us: shards(): lax.all_to_all(saved_input, 'ctx', split_axis=1, concat_axis=0, tiled=True)]
    all_to_all x3 -> x0, local copies, waits for them, and re-layouts: 17.9 us -> none  [the longest x1 11.4 us: shards(): lax.all_to_all(stacked, 'ctx', split_axis=0, concat_axis=1, tiled=True)]
    unnamed x7 -> x0, other arithmetic: 15.1 us -> none
  transfers between devices with their start and end apart: 5 -> 0, of which waited for: 4 -> 0; matrix products, arithmetic and copies ran while one was open for 3% -> 0% of each run, Pallas kernels for 0% -> 0%
where the time goes in v1:
time: 72.5 us; the launch traced here: 72.2 us
  blocking collectives  56.9 us (78%)
  Pallas kernels  11.4 us (16%)
  local copies, waits for them, and re-layouts  3.17 us (4%)
  between operations  0.73 us (1%)
    all_to_all x1, blocking collectives, shards(): lax.all_to_all(packed, ('dp', 'ctx'), split_axis=0, concat_axis=0, tiled=...  33.3 us
    all_to_all x1, blocking collectives, shards(): lax.all_to_all(results, ('dp', 'ctx'), split_axis=0, concat_axis=0, tiled...  23.6 us
    pallas_call x1, Pallas kernels, shards(): pl.pallas_call(functools.partial(convolve_kernel, group), out_shape=jax.S...  8.62 us
    unnamed x16, local copies, waits for them, and re-layouts  3.15 us
    pallas_call x1, Pallas kernels, shards(): pl.pallas_call(functools.partial(unpack_kernel, peers), out_shape=(jax.Sh...  2.25 us

profile of v1, /device:TPU:1, one launch (start us, length us, event | category | flops | bytes accessed | tf_op | source)
XLA Modules:
  0.0 72.2 jit_solution(997443628940418530)
XLA Ops:
  0.6 0.0 copy-start
  0.6 1.0 %copy-done = bf16[512,512]{1,0:T(8,128)(2,1)S(1)} copy-done((bf16[512,512]{1,0:T(8,128)(2,1)S(1)}, bf16[512,512]{1,0:T(8,128)(2,1)}, u32[]{:S(2)}) %copy-start) | copy-done | bytes 524312
  1.7 0.0 copy-start.1
  1.7 1.0 %copy-done.1 = bf16[1,512,512]{2,1,0:T(8,128)(2,1)S(1)} copy-done((bf16[1,512,512]{2,1,0:T(8,128)(2,1)S(1)}, bf16[1,512,512]{2,1,0:T(8,128)(2,1)}, u32[]{:S(2)}) %copy-start.1) | copy-done | bytes 524312
  2.7 0.0 copy-start.2
  2.7 1.0 %copy-done.2 = bf16[1,512,512]{2,1,0:T(8,128)(2,1)S(1)} copy-done((bf16[1,512,512]{2,1,0:T(8,128)(2,1)S(1)}, bf16[1,512,512]{2,1,0:T(8,128)(2,1)}, u32[]{:S(2)}) %copy-start.2) | copy-done | bytes 524312
  3.8 0.5 pack.1
  4.3 0.0 copy-start.3
  4.3 0.0 copy-start.4
  4.4 0.0 copy-start.5
  4.4 0.0 copy-start.6
  4.4 0.0 copy-start.7
  4.4 33.3 %all_to_all.10.in_ref = bf16[128,40,128]{2,1,0:T(8,128)(2,1)S(1)} all-to-all(bf16[128,40,128]{2,1,0:T(8,128)(2,1)S(1)} %pack.1), channel_id=1, replica_groups=mesh['dp'=2,'ctx'=64] {'dp','ctx'}, dimensions={0} | all-to-all | bytes 2621440 | tf_op jit(solution)/shard_map/all_to_all | solution.py:186
  37.7 0.0 copy-done.3
  37.7 0.0 copy-done.4
  37.7 0.0 copy-done.5
  37.7 0.0 copy-done.6
  37.7 0.0 copy-done.7
  37.7 8.6 %convolve.1 = bf16[128,32,128]{2,1,0:T(8,128)(2,1)S(1)} custom-call(bf16[128,40,128]{2,1,0:T(8,128)(2,1)S(1)} %all_to_all.10.in_ref, bf16[1024,256]{1,0:T(8,128)(2,1)S(1)} %copy-done.4, bf16[512,512]{1,0:T(8,128)(2,1)S(1)} %copy-done.3, bf16[512,256]{1,0:T(8,128)(2,1)S(1)} %copy-done.7, bf16[512,256]{1,0:T(8,128)(2,1)S(1)} %copy-done.6, f32[512,128]{1,0:T(8,128)S(1)} %copy-done.5), custom_call_target="tpu_custom_call" | custom-call | tf_op jit(solution)/shard_map/convolve/pallas_call | solution.py:187
  46.4 23.6 %all_to_all.11.in_ref = bf16[128,32,128]{2,1,0:T(8,128)(2,1)S(1)} all-to-all(bf16[128,32,128]{2,1,0:T(8,128)(2,1)S(1)} %convolve.1), channel_id=1, replica_groups=mesh['dp'=2,'ctx'=64] {'dp','ctx'}, dimensions={0} | all-to-all | bytes 2097152 | tf_op jit(solution)/shard_map/all_to_all | solution.py:200
  70.0 2.2 %unpack.1 = (bf16[512,512]{1,0:T(8,128)(2,1)}, f32[512,256]{1,0:T(8,128)}) custom-call(bf16[128,32,128]{2,1,0:T(8,128)(2,1)S(1)} %all_to_all.11.in_ref), custom_call_target="tpu_custom_call" | custom-call | tf_op jit(solution)/shard_map/unpack/pallas_call | solution.py:201
  (1 shorter events, 0.0 us)
Async XLA Ops:
  0.6 1.0 %copy-start = (bf16[512,512]{1,0:T(8,128)(2,1)S(1)}, bf16[512,512]{1,0:T(8,128)(2,1)}, u32[]{:S(2)}) copy-start(bf16[512,512]{1,0:T(8,128)(2,1)} %param.10) | copy-start | bytes 1572868
  1.7 1.0 %copy-start.1 = (bf16[1,512,512]{2,1,0:T(8,128)(2,1)S(1)}, bf16[1,512,512]{2,1,0:T(8,128)(2,1)}, u32[]{:S(2)}) copy-start(bf16[1,512,512]{2,1,0:T(8,128)(2,1)} %param.8) | copy-start | bytes 1572868
  2.7 1.0 %copy-start.2 = (bf16[1,512,512]{2,1,0:T(8,128)(2,1)S(1)}, bf16[1,512,512]{2,1,0:T(8,128)(2,1)}, u32[]{:S(2)}) copy-start(bf16[1,512,512]{2,1,0:T(8,128)(2,1)} %param.9) | copy-start | bytes 1572868
  4.3 33.4 %copy-start.3 = (bf16[512,512]{1,0:T(8,128)(2,1)S(1)}, bf16[512,512]{1,0:T(8,128)(2,1)}, u32[]{:S(2)}) copy-start(bf16[512,512]{1,0:T(8,128)(2,1)} %constant.23.clone.last_ref) | copy-start | bytes 1572868
  4.3 33.4 %copy-start.4 = (bf16[1024,256]{1,0:T(8,128)(2,1)S(1)}, bf16[1024,256]{1,0:T(8,128)(2,1)}, u32[]{:S(2)}) copy-start(bf16[1024,256]{1,0:T(8,128)(2,1)} %constant.22.clone.first_ref) | copy-start | bytes 1572868
  4.4 33.4 %copy-start.5 = (f32[512,128]{1,0:T(8,128)S(1)}, f32[512,128]{1,0:T(8,128)}, u32[]{:S(2)}) copy-start(f32[512,128]{1,0:T(8,128)} %constant.26.clone.turn_ref) | copy-start | bytes 786436
  4.4 33.3 %copy-start.6 = (bf16[512,256]{1,0:T(8,128)(2,1)S(1)}, bf16[512,256]{1,0:T(8,128)(2,1)}, u32[]{:S(2)}) copy-start(bf16[512,256]{1,0:T(8,128)(2,1)} %constant.25.clone.back_ref) | copy-start | bytes 786436
  4.4 33.3 %copy-start.7 = (bf16[512,256]{1,0:T(8,128)(2,1)S(1)}, bf16[512,256]{1,0:T(8,128)(2,1)}, u32[]{:S(2)}) copy-start(bf16[512,256]{1,0:T(8,128)(2,1)} %constant.24.clone.forth_ref) | copy-start | bytes 786436

commit v2 on v1

--- a/solution.py
+++ b/solution.py
@@ -59,35 +59,45 @@
     return high, (value - high.astype(F32)).astype(BF16)
 
 
-def pack_kernel(peers, dp_index, u_ref, g_ref, h_ref, out_ref, held):
-    blocks = u_ref.shape[0] // LANES
-    group = peers // 2
-
-    def place(ref, block, row):
-        flipped = ref[block * LANES : (block + 1) * LANES, :].astype(F32).T
-        for c in range(OWN):
-            held[pl.ds(row + c, peers, stride=40), :] = flipped[c * peers : (c + 1) * peers, :]
-
-    for q in range(blocks):
-        place(u_ref, q, OWN * q)
-        place(g_ref, q, 16 + OWN * q)
-    for q in range(2):
-        place(h_ref, q, 32 + OWN * q)
+def pack_kernel(peers, u_ref, g_ref, h_ref, out_ref, landed, taps_landed, held, sems):
+    share = taps_landed.shape[0]
+    own = pl.multiple_of(lax.axis_index("dp") * share, share)
+    arrivals = (
+        (pltpu.make_async_copy(u_ref, landed.at[0], sems.at[0]), landed.at[0], 0),
+        (pltpu.make_async_copy(g_ref, landed.at[1], sems.at[1]), landed.at[1], 16),
+        (pltpu.make_async_copy(h_ref.at[pl.ds(own, share), :], taps_landed, sems.at[2]), taps_landed, 32),
+    )
+    for copy, _, _ in arrivals:
+        copy.start()
+    for copy, block, first_row in arrivals:
+        copy.wait()
+        for q in range(block.shape[0] // LANES):
+            flipped = block[q * LANES : (q + 1) * LANES, :].astype(F32).T
+            for c in range(OWN):
+                row = first_row + OWN * q + c
+                held[pl.ds(row, peers, stride=40), :] = flipped[c * peers : (c + 1) * peers, :]
     out_ref[...] = held[...].reshape(peers, 40, LANES).astype(BF16)
 
 
-def unpack_kernel(peers, in_ref, input_ref, filter_ref, held):
+def unpack_kernel(peers, in_ref, input_ref, filter_ref, held, input_block, filter_block, sems):
     blocks = input_ref.shape[0] // LANES
     held[...] = in_ref[...].astype(F32).reshape(peers * 32, LANES)
+    leaving = []
     for q in range(blocks):
         rows = slice(q * LANES, (q + 1) * LANES)
         for c in range(OWN):
             piece = held[pl.ds(OWN * q + c, peers, stride=32), :]
-            input_ref[rows, c * peers : (c + 1) * peers] = piece.T.astype(BF16)
+            input_block[rows, c * peers : (c + 1) * peers] = piece.T.astype(BF16)
+        leaving.append(pltpu.make_async_copy(input_block.at[rows], input_ref.at[rows], sems.at[2 * q]))
+        leaving[-1].start()
         for c in range(OWN // 2):
             high = held[pl.ds(16 + 2 * q + c, peers, stride=32), :]
             low = held[pl.ds(24 + 2 * q + c, peers, stride=32), :]
-            filter_ref[rows, c * peers : (c + 1) * peers] = (high + low).T
+            filter_block[rows, c * peers : (c + 1) * peers] = (high + low).T
+        leaving.append(pltpu.make_async_copy(filter_block.at[rows], filter_ref.at[rows], sems.at[2 * q + 1]))
+        leaving[-1].start()
+    for copy in leaving:
+        copy.wait()
 
 
 def convolve_kernel(group, in_ref, first_ref, last_ref, forth_ref, back_ref, turn_ref, out_ref, u_held, g_held, h_held, in_grad, taps_grad):
@@ -175,14 +185,22 @@
     rows = seq // LANES
     constants = [jnp.asarray(table) for table in tables(seq)]
     params = pltpu.CompilerParams(vmem_limit_bytes=48 * 1024 * 1024)
-    own_taps = lax.dynamic_slice_in_dim(filter_taps, lax.axis_index("dp") * (local_len // 2), local_len // 2, 0)
+    local = pl.BlockSpec(memory_space=pltpu.VMEM)
+    far = pl.BlockSpec(memory_space=pltpu.HBM)
     packed = pl.pallas_call(
-        functools.partial(pack_kernel, peers, None),
+        functools.partial(pack_kernel, peers),
         out_shape=jax.ShapeDtypeStruct((peers, 40, LANES), BF16),
-        scratch_shapes=[pltpu.VMEM((peers * 40, LANES), F32)],
+        in_specs=[far] * 3,
+        out_specs=local,
+        scratch_shapes=[
+            pltpu.VMEM((2, local_len, chan_count), BF16),
+            pltpu.VMEM((local_len // 2, chan_count), BF16),
+            pltpu.VMEM((peers * 40, LANES), F32),
+            pltpu.SemaphoreType.DMA((3,)),
+        ],
         compiler_params=params,
         name="pack",
-    )(saved_input[0], output_grad[0], own_taps)
+    )(*[pltpu.with_memory_space_constraint(x, pltpu.HBM) for x in (saved_input[0], output_grad[0], filter_taps)])
     received = lax.all_to_all(packed, ("dp", "ctx"), split_axis=0, concat_axis=0, tiled=True)
     results = pl.pallas_call(
         functools.partial(convolve_kernel, group),
@@ -204,7 +222,14 @@
             jax.ShapeDtypeStruct((local_len, chan_count), BF16),
             jax.ShapeDtypeStruct((local_len, chan_count // 2), F32),
         ),
-        scratch_shapes=[pltpu.VMEM((peers * 32, LANES), F32)],
+        in_specs=[local],
+        out_specs=(far, far),
+        scratch_shapes=[
+            pltpu.VMEM((peers * 32, LANES), F32),
+            pltpu.VMEM((local_len, chan_count), BF16),
+            pltpu.VMEM((local_len, chan_count // 2), F32),
+            pltpu.SemaphoreType.DMA((2 * (local_len // LANES),)),
+        ],
         compiler_params=params,
         name="unpack",
     )(returned)

time: 72.5 us -> 70.3 us (0.970)
  local copies, waits for them, and re-layouts: 3.17 us -> 0.03 us
  Pallas kernels: 11.4 us -> 12.5 us
    unnamed x16 -> x10, local copies, waits for them, and re-layouts: 3.15 us -> 0.03 us
    pallas_call x1, Pallas kernels: 0.54 us -> 1.75 us  [shards(): pl.pallas_call(functools.partial(pack_kernel, peers), out_shape=jax.Shape...]
where the time goes in v2:
time: 70.3 us; the launch traced here: 70.1 us
  blocking collectives  56.9 us (81%)
  Pallas kernels  12.5 us (18%)
  between operations  0.71 us (1%)
    all_to_all x1, blocking collectives, shards(): lax.all_to_all(packed, ('dp', 'ctx'), split_axis=0, concat_axis=0, tiled=...  33.3 us
    all_to_all x1, blocking collectives, shards(): lax.all_to_all(results, ('dp', 'ctx'), split_axis=0, concat_axis=0, tiled...  23.6 us
    pallas_call x1, Pallas kernels, shards(): pl.pallas_call(functools.partial(convolve_kernel, group), out_shape=jax.S...  8.62 us
    pallas_call x1, Pallas kernels, shards(): pl.pallas_call(functools.partial(unpack_kernel, peers), out_shape=(jax.Sh...  2.09 us
    pallas_call x1, Pallas kernels, shards(): pl.pallas_call(functools.partial(pack_kernel, peers), out_shape=jax.Shape...  1.75 us

profile of v2, /device:TPU:1, one launch (start us, length us, event | category | flops | bytes accessed | tf_op | source)
XLA Modules:
  0.0 70.1 jit_solution(336838922920783618)
XLA Ops:
  0.6 1.8 %pack.1 = bf16[128,40,128]{2,1,0:T(8,128)(2,1)S(1)} custom-call(bf16[512,512]{1,0:T(8,128)(2,1)} %bitcast.3, bf16[512,512]{1,0:T(8,128)(2,1)} %bitcast.4, bf16[512,512]{1,0:T(8,128)(2,1)} %h_ref.1), custom_call_target="tpu_custom_call" | custom-call | tf_op jit(solution)/shard_map/pack/pallas_call | solution.py:190
  2.4 0.0 copy-start
  2.4 0.0 copy-start.1
  2.4 0.0 copy-start.2
  2.4 0.0 copy-start.3
  2.4 0.0 copy-start.4
  2.5 33.3 %all_to_all.10.in_ref = bf16[128,40,128]{2,1,0:T(8,128)(2,1)S(1)} all-to-all(bf16[128,40,128]{2,1,0:T(8,128)(2,1)S(1)} %pack.1), channel_id=1, replica_groups=mesh['dp'=2,'ctx'=64] {'dp','ctx'}, dimensions={0} | all-to-all | bytes 2621440 | tf_op jit(solution)/shard_map/all_to_all | solution.py:204
  35.8 0.0 copy-done
  35.8 0.0 copy-done.1
  35.8 0.0 copy-done.2
  35.8 0.0 copy-done.3
  35.8 0.0 copy-done.4
  35.8 8.6 %convolve.1 = bf16[128,32,128]{2,1,0:T(8,128)(2,1)S(1)} custom-call(bf16[128,40,128]{2,1,0:T(8,128)(2,1)S(1)} %all_to_all.10.in_ref, bf16[1024,256]{1,0:T(8,128)(2,1)S(1)} %copy-done.1, bf16[512,512]{1,0:T(8,128)(2,1)S(1)} %copy-done, bf16[512,256]{1,0:T(8,128)(2,1)S(1)} %copy-done.4, bf16[512,256]{1,0:T(8,128)(2,1)S(1)} %copy-done.3, f32[512,128]{1,0:T(8,128)S(1)} %copy-done.2), custom_call_target="tpu_custom_call" | custom-call | tf_op jit(solution)/shard_map/convolve/pallas_call | solution.py:205
  44.4 23.6 %all_to_all.11.in_ref = bf16[128,32,128]{2,1,0:T(8,128)(2,1)S(1)} all-to-all(bf16[128,32,128]{2,1,0:T(8,128)(2,1)S(1)} %convolve.1), channel_id=1, replica_groups=mesh['dp'=2,'ctx'=64] {'dp','ctx'}, dimensions={0} | all-to-all | bytes 2097152 | tf_op jit(solution)/shard_map/all_to_all | solution.py:218
  68.0 2.1 %unpack.1 = (bf16[512,512]{1,0:T(8,128)(2,1)}, f32[512,256]{1,0:T(8,128)}) custom-call(bf16[128,32,128]{2,1,0:T(8,128)(2,1)S(1)} %all_to_all.11.in_ref), custom_call_target="tpu_custom_call" | custom-call | tf_op jit(solution)/shard_map/unpack/pallas_call | solution.py:219
Async XLA Ops:
  2.4 33.4 %copy-start = (bf16[512,512]{1,0:T(8,128)(2,1)S(1)}, bf16[512,512]{1,0:T(8,128)(2,1)}, u32[]{:S(2)}) copy-start(bf16[512,512]{1,0:T(8,128)(2,1)} %constant.11.clone.last_ref) | copy-start | bytes 1572868
  2.4 33.4 %copy-start.1 = (bf16[1024,256]{1,0:T(8,128)(2,1)S(1)}, bf16[1024,256]{1,0:T(8,128)(2,1)}, u32[]{:S(2)}) copy-start(bf16[1024,256]{1,0:T(8,128)(2,1)} %constant.10.clone.first_ref) | copy-start | bytes 1572868
  2.4 33.4 %copy-start.2 = (f32[512,128]{1,0:T(8,128)S(1)}, f32[512,128]{1,0:T(8,128)}, u32[]{:S(2)}) copy-start(f32[512,128]{1,0:T(8,128)} %constant.14.clone.turn_ref) | copy-start | bytes 786436
  2.4 33.3 %copy-start.3 = (bf16[512,256]{1,0:T(8,128)(2,1)S(1)}, bf16[512,256]{1,0:T(8,128)(2,1)}, u32[]{:S(2)}) copy-start(bf16[512,256]{1,0:T(8,128)(2,1)} %constant.13.clone.back_ref) | copy-start | bytes 786436
  2.4 33.3 %copy-start.4 = (bf16[512,256]{1,0:T(8,128)(2,1)S(1)}, bf16[512,256]{1,0:T(8,128)(2,1)}, u32[]{:S(2)}) copy-start(bf16[512,256]{1,0:T(8,128)(2,1)} %constant.12.clone.forth_ref) | copy-start | bytes 786436

commit v3 on v2

--- a/solution.py
+++ b/solution.py
@@ -15,6 +15,7 @@
 F32 = jnp.float32
 OWN = 4
 BATCH = 2
+STEPS = 959.0
 
 
 def two_parts(matrix):
@@ -59,6 +60,41 @@
     return high, (value - high.astype(F32)).astype(BF16)
 
 
+def word(code, exponent):
+    negative = code >= 128.0
+    size = jnp.where(negative, code, code + 128.0) * (1 / 128) * jnp.exp2(exponent)
+    return jnp.where(negative, -size, size)
+
+
+def code_of(held_word):
+    size = jnp.abs(held_word)
+    exponent = jnp.floor(jnp.log2(size) + 0.002)
+    digits = jnp.floor(size * jnp.exp2(7.0 - exponent) + 0.5)
+    return jnp.where(held_word < 0.0, digits, digits - 128.0), exponent
+
+
+def encode(one, two):
+    top = jnp.maximum(jnp.maximum(jnp.abs(one), jnp.abs(two)), 2.0**-115)
+    exponent = jnp.floor(jnp.log2(top))
+    scale = jnp.exp2(-exponent)
+    one_code = jnp.floor(one * scale * STEPS + (2 * STEPS + 0.5))
+    two_code = jnp.floor(two * scale * STEPS + (2 * STEPS + 0.5))
+    coarse = jnp.floor(one_code * (1 / 16))
+    rest = two_code * 16.0 + (one_code - 16.0 * coarse)
+    upper = jnp.floor(rest * (1 / 256))
+    return word(coarse, exponent), word(rest - 256.0 * upper, upper - 120.0)
+
+
+def decode(first_word, second_word):
+    coarse, exponent = code_of(first_word)
+    lower, upper = code_of(second_word)
+    rest = (upper + 120.0) * 256.0 + lower
+    two_code = jnp.floor(rest * (1 / 16))
+    one_code = 16.0 * coarse + (rest - 16.0 * two_code)
+    scale = jnp.exp2(exponent) * (1 / STEPS)
+    return (one_code - 2 * STEPS) * scale, (two_code - 2 * STEPS) * scale
+
+
 def pack_kernel(peers, u_ref, g_ref, h_ref, out_ref, landed, taps_landed, held, sems):
     share = taps_landed.shape[0]
     own = pl.multiple_of(lax.axis_index("dp") * share, share)
@@ -81,19 +117,18 @@
 
 def unpack_kernel(peers, in_ref, input_ref, filter_ref, held, input_block, filter_block, sems):
     blocks = input_ref.shape[0] // LANES
-    held[...] = in_ref[...].astype(F32).reshape(peers * 32, LANES)
+    held[...] = in_ref[...].astype(F32).reshape(peers * 24, LANES)
     leaving = []
     for q in range(blocks):
         rows = slice(q * LANES, (q + 1) * LANES)
         for c in range(OWN):
-            piece = held[pl.ds(OWN * q + c, peers, stride=32), :]
+            piece = held[pl.ds(OWN * q + c, peers, stride=24), :]
             input_block[rows, c * peers : (c + 1) * peers] = piece.T.astype(BF16)
         leaving.append(pltpu.make_async_copy(input_block.at[rows], input_ref.at[rows], sems.at[2 * q]))
         leaving[-1].start()
-        for c in range(OWN // 2):
-            high = held[pl.ds(16 + 2 * q + c, peers, stride=32), :]
-            low = held[pl.ds(24 + 2 * q + c, peers, stride=32), :]
-            filter_block[rows, c * peers : (c + 1) * peers] = (high + low).T
+        words = [held[pl.ds(16 + 2 * q + c, peers, stride=24), :] for c in range(2)]
+        for c, piece in enumerate(decode(*words)):
+            filter_block[rows, c * peers : (c + 1) * peers] = piece.T
         leaving.append(pltpu.make_async_copy(filter_block.at[rows], filter_ref.at[rows], sems.at[2 * q + 1]))
         leaving[-1].start()
     for copy in leaving:
@@ -167,13 +202,11 @@
         result = backward(
             [correlate(grad_spec[0][i], signal_spec[0][i]) + correlate(grad_spec[1][i], signal_spec[1][i]) for i in range(2)]
         )
-        for i in range(2):
-            taps_grad[half, pl.ds(i, rows, stride=2), :] = result[:, i * LANES : (i + 1) * LANES]
+        for i, coded in enumerate(encode(result[:, :LANES], result[:, LANES:])):
+            taps_grad[half, pl.ds(i, rows, stride=2), :] = coded
     for d in range(2):
-        taps_out = taps_grad[d].reshape(group, 8, LANES)
-        high = taps_out.astype(BF16).astype(F32)
         out_ref[d * group : (d + 1) * group] = jnp.concatenate(
-            [in_grad[d].reshape(group, 16, LANES), high, taps_out - high], axis=1
+            [in_grad[d].reshape(group, 16, LANES), taps_grad[d].reshape(group, 8, LANES)], axis=1
         ).astype(BF16)
 
 
@@ -204,7 +237,7 @@
     received = lax.all_to_all(packed, ("dp", "ctx"), split_axis=0, concat_axis=0, tiled=True)
     results = pl.pallas_call(
         functools.partial(convolve_kernel, group),
-        out_shape=jax.ShapeDtypeStruct((peers, 32, LANES), BF16),
+        out_shape=jax.ShapeDtypeStruct((peers, 24, LANES), BF16),
         scratch_shapes=[
             pltpu.VMEM((BATCH, group * 16, LANES), F32),
             pltpu.VMEM((BATCH, group * 16, LANES), F32),
@@ -225,7 +258,7 @@
         in_specs=[local],
         out_specs=(far, far),
         scratch_shapes=[
-            pltpu.VMEM((peers * 32, LANES), F32),
+            pltpu.VMEM((peers * 24, LANES), F32),
             pltpu.VMEM((local_len, chan_count), BF16),
             pltpu.VMEM((local_len, chan_count // 2), F32),
             pltpu.SemaphoreType.DMA((2 * (local_len // LANES),)),

time: 70.3 us -> 67 us (0.953)
  blocking collectives: 56.9 us -> 54.1 us
    all_to_all x1, blocking collectives: 23.6 us -> 20.8 us  [shards(): lax.all_to_all(results, ('dp', 'ctx'), split_axis=0, concat_axis=0, tiled...]
where the time goes in v3:
time: 67 us; the launch traced here: 66.9 us
  blocking collectives  54.1 us (81%)
  Pallas kernels  12 us (18%)
  between operations  0.7 us (1%)
    all_to_all x1, blocking collectives, shards(): lax.all_to_all(packed, ('dp', 'ctx'), split_axis=0, concat_axis=0, tiled=...  33.3 us
    all_to_all x1, blocking collectives, shards(): lax.all_to_all(results, ('dp', 'ctx'), split_axis=0, concat_axis=0, tiled...  20.8 us
    pallas_call x1, Pallas kernels, shards(): pl.pallas_call(functools.partial(convolve_kernel, group), out_shape=jax.S...  8.79 us
    pallas_call x1, Pallas kernels, shards(): pl.pallas_call(functools.partial(pack_kernel, peers), out_shape=jax.Shape...  1.75 us
    pallas_call x1, Pallas kernels, shards(): pl.pallas_call(functools.partial(unpack_kernel, peers), out_shape=(jax.Sh...  1.45 us

profile of v3, /device:TPU:1, one launch (start us, length us, event | category | flops | bytes accessed | tf_op | source)
XLA Modules:
  0.0 66.9 jit_solution(8521251865188232769)
XLA Ops:
  0.6 1.8 %pack.1 = bf16[128,40,128]{2,1,0:T(8,128)(2,1)S(1)} custom-call(bf16[512,512]{1,0:T(8,128)(2,1)} %bitcast.3, bf16[512,512]{1,0:T(8,128)(2,1)} %bitcast.4, bf16[512,512]{1,0:T(8,128)(2,1)} %h_ref.1), custom_call_target="tpu_custom_call" | custom-call | tf_op jit(solution)/shard_map/pack/pallas_call | solution.py:223
  2.4 0.0 copy-start
  2.4 0.0 copy-start.1
  2.4 0.0 copy-start.2
  2.4 0.0 copy-start.3
  2.4 0.0 copy-start.4
  2.5 33.3 %all_to_all.10.in_ref = bf16[128,40,128]{2,1,0:T(8,128)(2,1)S(1)} all-to-all(bf16[128,40,128]{2,1,0:T(8,128)(2,1)S(1)} %pack.1), channel_id=1, replica_groups=mesh['dp'=2,'ctx'=64] {'dp','ctx'}, dimensions={0} | all-to-all | bytes 2621440 | tf_op jit(solution)/shard_map/all_to_all | solution.py:237
  35.8 0.0 copy-done
  35.8 0.0 copy-done.1
  35.8 0.0 copy-done.2
  35.8 0.0 copy-done.3
  35.8 0.0 copy-done.4
  35.8 8.8 %convolve.1 = bf16[128,24,128]{2,1,0:T(8,128)(2,1)S(1)} custom-call(bf16[128,40,128]{2,1,0:T(8,128)(2,1)S(1)} %all_to_all.10.in_ref, bf16[1024,256]{1,0:T(8,128)(2,1)S(1)} %copy-done.1, bf16[512,512]{1,0:T(8,128)(2,1)S(1)} %copy-done, bf16[512,256]{1,0:T(8,128)(2,1)S(1)} %copy-done.4, bf16[512,256]{1,0:T(8,128)(2,1)S(1)} %copy-done.3, f32[512,128]{1,0:T(8,128)S(1)} %copy-done.2), custom_call_target="tpu_custom_call" | custom-call | tf_op jit(solution)/shard_map/convolve/pallas_call | solution.py:238
  44.6 20.8 %all_to_all.11.in_ref = bf16[128,24,128]{2,1,0:T(8,128)(2,1)S(1)} all-to-all(bf16[128,24,128]{2,1,0:T(8,128)(2,1)S(1)} %convolve.1), channel_id=1, replica_groups=mesh['dp'=2,'ctx'=64] {'dp','ctx'}, dimensions={0} | all-to-all | bytes 1572864 | tf_op jit(solution)/shard_map/all_to_all | solution.py:251
  65.4 1.4 %unpack.1 = (bf16[512,512]{1,0:T(8,128)(2,1)}, f32[512,256]{1,0:T(8,128)}) custom-call(bf16[128,24,128]{2,1,0:T(8,128)(2,1)S(1)} %all_to_all.11.in_ref), custom_call_target="tpu_custom_call" | custom-call | tf_op jit(solution)/shard_map/unpack/pallas_call | solution.py:252
Async XLA Ops:
  2.4 33.4 %copy-start = (bf16[512,512]{1,0:T(8,128)(2,1)S(1)}, bf16[512,512]{1,0:T(8,128)(2,1)}, u32[]{:S(2)}) copy-start(bf16[512,512]{1,0:T(8,128)(2,1)} %constant.11.clone.last_ref) | copy-start | bytes 1572868
  2.4 33.4 %copy-start.1 = (bf16[1024,256]{1,0:T(8,128)(2,1)S(1)}, bf16[1024,256]{1,0:T(8,128)(2,1)}, u32[]{:S(2)}) copy-start(bf16[1024,256]{1,0:T(8,128)(2,1)} %constant.10.clone.first_ref) | copy-start | bytes 1572868
  2.4 33.4 %copy-start.2 = (f32[512,128]{1,0:T(8,128)S(1)}, f32[512,128]{1,0:T(8,128)}, u32[]{:S(2)}) copy-start(f32[512,128]{1,0:T(8,128)} %constant.14.clone.turn_ref) | copy-start | bytes 786436
  2.4 33.3 %copy-start.3 = (bf16[512,256]{1,0:T(8,128)(2,1)S(1)}, bf16[512,256]{1,0:T(8,128)(2,1)}, u32[]{:S(2)}) copy-start(bf16[512,256]{1,0:T(8,128)(2,1)} %constant.13.clone.back_ref) | copy-start | bytes 786436
  2.4 33.3 %copy-start.4 = (bf16[512,256]{1,0:T(8,128)(2,1)S(1)}, bf16[512,256]{1,0:T(8,128)(2,1)}, u32[]{:S(2)}) copy-start(bf16[512,256]{1,0:T(8,128)(2,1)} %constant.12.clone.forth_ref) | copy-start | bytes 786436

commit v4 on v3

--- a/solution.py
+++ b/solution.py
@@ -24,6 +24,11 @@
     return high, low
 
 
+def three_parts(matrix, axis):
+    high, low = two_parts(matrix)
+    return np.concatenate([high, high, low], axis=axis)
+
+
 def turn(numerator, period):
     phase = (numerator % period) * (2.0 * math.pi / period)
     return np.cos(phase), np.sin(phase)
@@ -31,23 +36,25 @@
 
 @functools.cache
 def tables(seq):
-    rows = seq // LANES
+    rows = seq // (2 * LANES)
     k1 = np.arange(rows, dtype=np.int64)[:, None]
     a = np.arange(rows, dtype=np.int64)[None, :]
     r = np.arange(LANES, dtype=np.int64)
     cos_a, sin_a = turn((4 * k1 + 1) * a, 4 * rows)
     first = np.concatenate([cos_a, -sin_a], axis=0)
     last = np.concatenate([cos_a.T, -sin_a.T], axis=1) / seq
-    cos_t, sin_t = turn((4 * k1 + 1) * r[None, :], 4 * seq)
+    cos_t, sin_t = turn((4 * k1 + 1) * np.arange(2 * LANES, dtype=np.int64)[None, :], 4 * seq)
+    cos_h, sin_h = turn(r, 2 * LANES)
     cos_r, sin_r = turn(r[:, None] * r[None, :], LANES)
     forth = np.block([[cos_r, -sin_r], [sin_r, cos_r]])
     back = np.block([[cos_r, sin_r], [-sin_r, cos_r]])
+    halves = np.concatenate([np.tile(cos_h, (8, 1)), np.tile(sin_h, (8, 1))], axis=1)
     return (
-        np.concatenate(two_parts(first), axis=0),
-        np.concatenate(two_parts(last), axis=0),
-        np.concatenate(two_parts(forth), axis=0),
-        np.concatenate(two_parts(back), axis=0),
-        np.concatenate([cos_t, sin_t], axis=0).astype(np.float32),
+        np.concatenate(two_parts(first), axis=1),
+        three_parts(last, 1),
+        three_parts(forth, 0),
+        three_parts(back, 0),
+        np.concatenate([cos_t, sin_t, halves], axis=0).astype(np.float32),
     )
 
 
@@ -58,6 +65,21 @@
 def split(value):
     high = value.astype(BF16)
     return high, (value - high.astype(F32)).astype(BF16)
+
+
+def stack(value, axis):
+    high, low = split(value)
+    return jnp.concatenate([high, low, high], axis=axis)
+
+
+def interleave(tasks, at_once):
+    waiting, active = list(tasks), []
+    while waiting or active:
+        while waiting and len(active) < at_once:
+            active.append(waiting.pop(0))
+        for task in list(active):
+            if next(task, "over") == "over":
+                active.remove(task)
 
 
 def word(code, exponent):
@@ -136,74 +158,95 @@
 
 
 def convolve_kernel(group, in_ref, first_ref, last_ref, forth_ref, back_ref, turn_ref, out_ref, u_held, g_held, h_held, in_grad, taps_grad):
-    rows = group * OWN
+    rows = 2 * group
     for b in range(BATCH):
         got = in_ref[b * group : (b + 1) * group].astype(F32)
         u_held[b] = got[:, 0:16].reshape(group * 16, LANES)
         g_held[b] = got[:, 16:32].reshape(group * 16, LANES)
     taps = [in_ref[b * group : (b + 1) * group].astype(F32)[:, 32:40] for b in range(BATCH)]
     h_held[0] = jnp.concatenate(taps, axis=1).reshape(group * 16, LANES)
-    turn_cos = turn_ref[0:rows, :]
-    turn_sin = turn_ref[rows : 2 * rows, :]
-
-    def forward(held, b, channels):
-        pair = jnp.concatenate(
-            [held[b, pl.ds(c, rows, stride=OWN), :].astype(BF16) for c in channels], axis=1
+
+    def columns(value):
+        return value[:, :LANES], value[:, LANES:]
+
+    def turns():
+        turn_cos = columns(turn_ref[0:rows, :])
+        turn_sin = columns(turn_ref[rows : 2 * rows, :])
+        half_cos, half_sin = columns(turn_ref[2 * rows : 2 * rows + 1, :])
+        return turn_cos, turn_sin, half_cos, half_sin
+
+    spectra, finished = {}, {}
+
+    def forward(name, held, b, c):
+        values = jnp.concatenate(
+            [held[b, pl.ds(OWN * q + c, rows, stride=2 * OWN), :].astype(BF16) for q in range(2)], axis=1
         )
-        both = dot(first_ref[0 : 2 * rows, :], pair) + dot(first_ref[2 * rows : 4 * rows, :], pair)
-        spectra = []
-        for i in range(len(channels)):
-            lanes = slice(i * LANES, (i + 1) * LANES)
-            real, imag = both[0:rows, lanes], both[rows : 2 * rows, lanes]
-            turned = jnp.concatenate(
-                [real * turn_cos + imag * turn_sin, imag * turn_cos - real * turn_sin], axis=1
-            )
-            spectra.append(across(turned, forth_ref))
-        return spectra
-
-    def across(value, matrix_ref):
-        high, low = split(value)
-        width = 2 * LANES
-        return (
-            dot(high, matrix_ref[0:width, :])
-            + dot(low, matrix_ref[0:width, :])
-            + dot(high, matrix_ref[width : 2 * width, :])
+        both = dot(first_ref[...], jnp.concatenate([values, values], axis=0))
+        yield
+        turn_cos, turn_sin, half_cos, half_sin = turns()
+        turned = []
+        for q in range(2):
+            real, imag = columns(both[0:rows])[q], columns(both[rows : 2 * rows])[q]
+            turned.append((real * turn_cos[q] + imag * turn_sin[q], imag * turn_cos[q] - real * turn_sin[q]))
+        sum_re, sum_im = turned[0][0] + turned[1][0], turned[0][1] + turned[1][1]
+        off_re, off_im = turned[0][0] - turned[1][0], turned[0][1] - turned[1][1]
+        even = jnp.concatenate([sum_re, sum_im], axis=1)
+        odd = jnp.concatenate(
+            [off_re * half_cos + off_im * half_sin, off_im * half_cos - off_re * half_sin], axis=1
         )
-
-    def parts(spectrum):
-        return spectrum[:, :LANES], spectrum[:, LANES:]
-
-    def correlate(left, right):
-        left_re, left_im = parts(left)
-        right_re, right_im = parts(right)
+        spectra[name, c] = dot(stack(jnp.concatenate([even, odd], axis=0), 1), forth_ref[...])
+        yield
+
+    def correlate(left, right, c):
+        left_re, left_im = columns(spectra[left, c])
+        right_re, right_im = columns(spectra[right, c])
         return jnp.concatenate(
             [left_re * right_re + left_im * right_im, left_im * right_re - left_re * right_im], axis=1
         )
 
-    def backward(products):
+    def backward(pairs, c, store):
+        while not all((name, c) in spectra for pair in pairs for name in pair):
+            yield
+        product = functools.reduce(jnp.add, [correlate(left, right, c) for left, right in pairs])
+        spread = dot(stack(product, 1), back_ref[...])
+        yield
+        turn_cos, turn_sin, half_cos, half_sin = turns()
+        even_re, even_im = columns(spread[0:rows])
+        real, imag = columns(spread[rows : 2 * rows])
+        odd_re, odd_im = real * half_cos - imag * half_sin, imag * half_cos + real * half_sin
         reals, imags = [], []
-        for product in products:
-            real, imag = parts(across(product, back_ref))
-            reals.append(real * turn_cos - imag * turn_sin)
-            imags.append(imag * turn_cos + real * turn_sin)
-        stacked = jnp.concatenate([jnp.concatenate(reals, axis=1), jnp.concatenate(imags, axis=1)], axis=0)
-        high, low = split(stacked)
-        return dot(last_ref[0:rows, :], high) + dot(last_ref[0:rows, :], low) + dot(last_ref[rows : 2 * rows, :], high)
-
+        for q, (real, imag) in enumerate(((even_re + odd_re, even_im + odd_im), (even_re - odd_re, even_im - odd_im))):
+            reals.append(real * turn_cos[q] - imag * turn_sin[q])
+            imags.append(imag * turn_cos[q] + real * turn_sin[q])
+        turned = jnp.concatenate([jnp.concatenate(reals, axis=1), jnp.concatenate(imags, axis=1)], axis=0)
+        result = dot(last_ref[...], stack(turned, 0))
+        yield
+        store(result, c)
+
+    def store_input(b):
+        def store(result, c):
+            for q in range(2):
+                in_grad[b, pl.ds(OWN * q + c, rows, stride=2 * OWN), :] = columns(result)[q]
+
+        return store
+
+    def store_taps(result, c):
+        finished[c] = result
+        half = c // 2
+        if 2 * half in finished and 2 * half + 1 in finished:
+            for i, coded in enumerate(encode(finished[2 * half], finished[2 * half + 1])):
+                for q in range(2):
+                    taps_grad[half, pl.ds(2 * q + i, rows, stride=4), :] = columns(coded)[q]
+
+    tasks = []
     for half in range(2):
         channels = (2 * half, 2 * half + 1)
-        taps_spec = forward(h_held, 0, channels)
-        grad_spec = [forward(g_held, b, channels) for b in range(BATCH)]
+        for name, held, b in (("g0", g_held, 0), ("g1", g_held, 1), ("h", h_held, 0), ("u0", u_held, 0), ("u1", u_held, 1)):
+            tasks += [forward(name, held, b, c) for c in channels]
         for b in range(BATCH):
-            result = backward([correlate(grad_spec[b][i], taps_spec[i]) for i in range(2)])
-            for i in range(2):
-                in_grad[b, pl.ds(channels[i], rows, stride=OWN), :] = result[:, i * LANES : (i + 1) * LANES]
-        signal_spec = [forward(u_held, b, channels) for b in range(BATCH)]
-        result = backward(
-            [correlate(grad_spec[0][i], signal_spec[0][i]) + correlate(grad_spec[1][i], signal_spec[1][i]) for i in range(2)]
-        )
-        for i, coded in enumerate(encode(result[:, :LANES], result[:, LANES:])):
-            taps_grad[half, pl.ds(i, rows, stride=2), :] = coded
+            tasks += [backward([(f"g{b}", "h")], c, store_input(b)) for c in channels]
+        tasks += [backward([("g0", "u0"), ("g1", "u1")], c, store_taps) for c in channels]
+    interleave(tasks, 5)
     for d in range(2):
         out_ref[d * group : (d + 1) * group] = jnp.concatenate(
             [in_grad[d].reshape(group, 16, LANES), taps_grad[d].reshape(group, 8, LANES)], axis=1
@@ -215,7 +258,6 @@
     peers = 2 * group
     local_len, chan_count = filter_taps.shape
     seq = group * local_len
-    rows = seq // LANES
     constants = [jnp.asarray(table) for table in tables(seq)]
     params = pltpu.CompilerParams(vmem_limit_bytes=48 * 1024 * 1024)
     local = pl.BlockSpec(memory_space=pltpu.VMEM)

time: 67 us -> 65.9 us (0.984)
  Pallas kernels: 12 us -> 10.9 us
    pallas_call x1, Pallas kernels: 8.79 us -> 7.67 us  [shards(): pl.pallas_call(functools.partial(convolve_kernel, group), out_shape=jax.S...]
where the time goes in v4:
time: 65.9 us; the launch traced here: 65.8 us
  blocking collectives  54.2 us (82%)
  Pallas kernels  10.9 us (17%)
  between operations  0.7 us (1%)
    all_to_all x1, blocking collectives, shards(): lax.all_to_all(packed, ('dp', 'ctx'), split_axis=0, concat_axis=0, tiled=...  33.3 us
    all_to_all x1, blocking collectives, shards(): lax.all_to_all(results, ('dp', 'ctx'), split_axis=0, concat_axis=0, tiled...  20.8 us
    pallas_call x1, Pallas kernels, shards(): pl.pallas_call(functools.partial(convolve_kernel, group), out_shape=jax.S...  7.67 us
    pallas_call x1, Pallas kernels, shards(): pl.pallas_call(functools.partial(pack_kernel, peers), out_shape=jax.Shape...  1.75 us
    pallas_call x1, Pallas kernels, shards(): pl.pallas_call(functools.partial(unpack_kernel, peers), out_shape=(jax.Sh...  1.45 us

profile of v4, /device:TPU:1, one launch (start us, length us, event | category | flops | bytes accessed | tf_op | source)
XLA Modules:
  0.0 65.8 jit_solution(13018650511648962241)
XLA Ops:
  0.6 1.8 %pack.1 = bf16[128,40,128]{2,1,0:T(8,128)(2,1)S(1)} custom-call(bf16[512,512]{1,0:T(8,128)(2,1)} %bitcast.3, bf16[512,512]{1,0:T(8,128)(2,1)} %bitcast.4, bf16[512,512]{1,0:T(8,128)(2,1)} %h_ref.1), custom_call_target="tpu_custom_call" | custom-call | tf_op jit(solution)/shard_map/pack/pallas_call | solution.py:265
  2.4 0.0 copy-start
  2.4 0.0 copy-start.1
  2.4 0.0 copy-start.2
  2.4 0.0 copy-start.3
  2.4 0.0 copy-start.4
  2.5 33.3 %all_to_all.10.in_ref = bf16[128,40,128]{2,1,0:T(8,128)(2,1)S(1)} all-to-all(bf16[128,40,128]{2,1,0:T(8,128)(2,1)S(1)} %pack.1), channel_id=1, replica_groups=mesh['dp'=2,'ctx'=64] {'dp','ctx'}, dimensions={0} | all-to-all | bytes 2621440 | tf_op jit(solution)/shard_map/all_to_all | solution.py:279
  35.8 0.0 copy-done
  35.8 0.0 copy-done.1
  35.8 0.0 copy-done.2
  35.8 0.0 copy-done.3
  35.8 0.0 copy-done.4
  35.8 7.7 %convolve.1 = bf16[128,24,128]{2,1,0:T(8,128)(2,1)S(1)} custom-call(bf16[128,40,128]{2,1,0:T(8,128)(2,1)S(1)} %all_to_all.10.in_ref, bf16[256,256]{1,0:T(8,128)(2,1)S(1)} %copy-done.4, bf16[128,768]{1,0:T(8,128)(2,1)S(1)} %copy-done.3, bf16[768,256]{1,0:T(8,128)(2,1)S(1)} %copy-done.1, bf16[768,256]{1,0:T(8,128)(2,1)S(1)} %copy-done, f32[264,256]{1,0:T(8,128)S(1)} %copy-done.2), custom_call_target="tpu_custom_call" | custom-call | tf_op jit(solution)/shard_map/convolve/pallas_call | solution.py:280
  43.5 20.8 %all_to_all.11.in_ref = bf16[128,24,128]{2,1,0:T(8,128)(2,1)S(1)} all-to-all(bf16[128,24,128]{2,1,0:T(8,128)(2,1)S(1)} %convolve.1), channel_id=1, replica_groups=mesh['dp'=2,'ctx'=64] {'dp','ctx'}, dimensions={0} | all-to-all | bytes 1572864 | tf_op jit(solution)/shard_map/all_to_all | solution.py:293
  64.3 1.4 %unpack.1 = (bf16[512,512]{1,0:T(8,128)(2,1)}, f32[512,256]{1,0:T(8,128)}) custom-call(bf16[128,24,128]{2,1,0:T(8,128)(2,1)S(1)} %all_to_all.11.in_ref), custom_call_target="tpu_custom_call" | custom-call | tf_op jit(solution)/shard_map/unpack/pallas_call | solution.py:294
Async XLA Ops:
  2.4 33.4 %copy-start = (bf16[768,256]{1,0:T(8,128)(2,1)S(1)}, bf16[768,256]{1,0:T(8,128)(2,1)}, u32[]{:S(2)}) copy-start(bf16[768,256]{1,0:T(8,128)(2,1)} %constant.13.clone.back_ref) | copy-start | bytes 1179652
  2.4 33.4 %copy-start.1 = (bf16[768,256]{1,0:T(8,128)(2,1)S(1)}, bf16[768,256]{1,0:T(8,128)(2,1)}, u32[]{:S(2)}) copy-start(bf16[768,256]{1,0:T(8,128)(2,1)} %constant.12.clone.forth_ref) | copy-start | bytes 1179652
  2.4 33.4 %copy-start.2 = (f32[264,256]{1,0:T(8,128)S(1)}, f32[264,256]{1,0:T(8,128)}, u32[]{:S(2)}) copy-start(f32[264,256]{1,0:T(8,128)} %constant.14.clone.turn_ref) | copy-start | bytes 811012
  2.4 33.3 %copy-start.3 = (bf16[128,768]{1,0:T(8,128)(2,1)S(1)}, bf16[128,768]{1,0:T(8,128)(2,1)}, u32[]{:S(2)}) copy-start(bf16[128,768]{1,0:T(8,128)(2,1)} %constant.11.clone.last_ref) | copy-start | bytes 589828
  2.4 33.3 %copy-start.4 = (bf16[256,256]{1,0:T(8,128)(2,1)S(1)}, bf16[256,256]{1,0:T(8,128)(2,1)}, u32[]{:S(2)}) copy-start(bf16[256,256]{1,0:T(8,128)(2,1)} %constant.10.clone.first_ref) | copy-start | bytes 393220

commit v5 on v4

--- a/solution.py
+++ b/solution.py
@@ -40,21 +40,21 @@
     k1 = np.arange(rows, dtype=np.int64)[:, None]
     a = np.arange(rows, dtype=np.int64)[None, :]
     r = np.arange(LANES, dtype=np.int64)
-    cos_a, sin_a = turn((4 * k1 + 1) * a, 4 * rows)
-    first = np.concatenate([cos_a, -sin_a], axis=0)
-    last = np.concatenate([cos_a.T, -sin_a.T], axis=1) / seq
-    cos_t, sin_t = turn((4 * k1 + 1) * np.arange(2 * LANES, dtype=np.int64)[None, :], 4 * seq)
-    cos_h, sin_h = turn(r, 2 * LANES)
+    first, last = [], []
+    for q in range(2):
+        cos_a, sin_a = turn((4 * k1 + 1) * (2 * a + q), 8 * rows)
+        first.append(np.concatenate(two_parts(np.concatenate([cos_a, -sin_a], axis=0)), axis=1))
+        last.append(three_parts(np.concatenate([cos_a.T, -sin_a.T], axis=1) / seq, 1))
+    turns = [np.concatenate(turn((4 * (k1 + m * rows) + 1) * r[None, :], 4 * seq), axis=1) for m in range(2)]
     cos_r, sin_r = turn(r[:, None] * r[None, :], LANES)
     forth = np.block([[cos_r, -sin_r], [sin_r, cos_r]])
     back = np.block([[cos_r, sin_r], [-sin_r, cos_r]])
-    halves = np.concatenate([np.tile(cos_h, (8, 1)), np.tile(sin_h, (8, 1))], axis=1)
     return (
-        np.concatenate(two_parts(first), axis=1),
-        three_parts(last, 1),
+        np.concatenate(first, axis=0),
+        np.concatenate(last, axis=0),
         three_parts(forth, 0),
         three_parts(back, 0),
-        np.concatenate([cos_t, sin_t, halves], axis=0).astype(np.float32),
+        np.concatenate(turns, axis=0).astype(np.float32),
     )
 
 
@@ -169,32 +169,28 @@
     def columns(value):
         return value[:, :LANES], value[:, LANES:]
 
-    def turns():
-        turn_cos = columns(turn_ref[0:rows, :])
-        turn_sin = columns(turn_ref[rows : 2 * rows, :])
-        half_cos, half_sin = columns(turn_ref[2 * rows : 2 * rows + 1, :])
-        return turn_cos, turn_sin, half_cos, half_sin
-
-    spectra, finished = {}, {}
-
-    def forward(name, held, b, c):
-        values = jnp.concatenate(
-            [held[b, pl.ds(OWN * q + c, rows, stride=2 * OWN), :].astype(BF16) for q in range(2)], axis=1
-        )
-        both = dot(first_ref[...], jnp.concatenate([values, values], axis=0))
+    def turns(m):
+        return columns(turn_ref[m * rows : (m + 1) * rows, :])
+
+    spectra = {}
+
+    def forward(name, held, b, channels):
+        both = []
+        for q in range(2):
+            values = jnp.concatenate(
+                [held[b, pl.ds(OWN * q + c, rows, stride=2 * OWN), :].astype(BF16) for c in channels], axis=1
+            )
+            both.append(dot(first_ref[2 * rows * q : 2 * rows * (q + 1), :], jnp.concatenate([values, values], axis=0)))
         yield
-        turn_cos, turn_sin, half_cos, half_sin = turns()
-        turned = []
-        for q in range(2):
-            real, imag = columns(both[0:rows])[q], columns(both[rows : 2 * rows])[q]
-            turned.append((real * turn_cos[q] + imag * turn_sin[q], imag * turn_cos[q] - real * turn_sin[q]))
-        sum_re, sum_im = turned[0][0] + turned[1][0], turned[0][1] + turned[1][1]
-        off_re, off_im = turned[0][0] - turned[1][0], turned[0][1] - turned[1][1]
-        even = jnp.concatenate([sum_re, sum_im], axis=1)
-        odd = jnp.concatenate(
-            [off_re * half_cos + off_im * half_sin, off_im * half_cos - off_re * half_sin], axis=1
-        )
-        spectra[name, c] = dot(stack(jnp.concatenate([even, odd], axis=0), 1), forth_ref[...])
+        sums = (both[0] + both[1], both[0] - both[1])
+        for i, c in enumerate(channels):
+            turned = []
+            for m in range(2):
+                turn_cos, turn_sin = turns(m)
+                real, imag = columns(sums[m][0:rows])[i], columns(sums[m][rows : 2 * rows])[i]
+                turned.append(jnp.concatenate([real * turn_cos + imag * turn_sin, imag * turn_cos - real * turn_sin], axis=1))
+            spectra[name, c] = dot(stack(jnp.concatenate(turned, axis=0), 1), forth_ref[...])
+            yield
         yield
 
     def correlate(left, right, c):
@@ -204,49 +200,57 @@
             [left_re * right_re + left_im * right_im, left_im * right_re - left_re * right_im], axis=1
         )
 
-    def backward(pairs, c, store):
-        while not all((name, c) in spectra for pair in pairs for name in pair):
+    def backward(pairs, channels, store):
+        while not all((name, c) in spectra for pair in pairs for name in pair for c in channels):
             yield
-        product = functools.reduce(jnp.add, [correlate(left, right, c) for left, right in pairs])
-        spread = dot(stack(product, 1), back_ref[...])
+        spread = []
+        for c in channels:
+            product = functools.reduce(jnp.add, [correlate(left, right, c) for left, right in pairs])
+            spread.append(dot(stack(product, 1), back_ref[...]))
+            yield
         yield
-        turn_cos, turn_sin, half_cos, half_sin = turns()
-        even_re, even_im = columns(spread[0:rows])
-        real, imag = columns(spread[rows : 2 * rows])
-        odd_re, odd_im = real * half_cos - imag * half_sin, imag * half_cos + real * half_sin
-        reals, imags = [], []
-        for q, (real, imag) in enumerate(((even_re + odd_re, even_im + odd_im), (even_re - odd_re, even_im - odd_im))):
-            reals.append(real * turn_cos[q] - imag * turn_sin[q])
-            imags.append(imag * turn_cos[q] + real * turn_sin[q])
-        turned = jnp.concatenate([jnp.concatenate(reals, axis=1), jnp.concatenate(imags, axis=1)], axis=0)
-        result = dot(last_ref[...], stack(turned, 0))
+        terms = []
+        for one in spread:
+            for m in range(2):
+                turn_cos, turn_sin = turns(m)
+                real, imag = columns(one[m * rows : (m + 1) * rows])
+                terms.append(jnp.concatenate([real * turn_cos - imag * turn_sin, imag * turn_cos + real * turn_sin], axis=0))
+        results = []
+        for q in range(2):
+            turned = jnp.concatenate([terms[2 * i] + terms[2 * i + 1] if q == 0 else terms[2 * i] - terms[2 * i + 1] for i in range(2)], axis=1)
+            results.append(dot(last_ref[rows * q : rows * (q + 1), :], stack(turned, 0)))
+            yield
         yield
-        store(result, c)
+        store(results, channels)
 
     def store_input(b):
-        def store(result, c):
+        def store(results, channels):
             for q in range(2):
-                in_grad[b, pl.ds(OWN * q + c, rows, stride=2 * OWN), :] = columns(result)[q]
+                for i, c in enumerate(channels):
+                    in_grad[b, pl.ds(OWN * q + c, rows, stride=2 * OWN), :] = columns(results[q])[i]
 
         return store
 
-    def store_taps(result, c):
-        finished[c] = result
-        half = c // 2
-        if 2 * half in finished and 2 * half + 1 in finished:
-            for i, coded in enumerate(encode(finished[2 * half], finished[2 * half + 1])):
-                for q in range(2):
-                    taps_grad[half, pl.ds(2 * q + i, rows, stride=4), :] = columns(coded)[q]
-
-    tasks = []
-    for half in range(2):
-        channels = (2 * half, 2 * half + 1)
-        for name, held, b in (("g0", g_held, 0), ("g1", g_held, 1), ("h", h_held, 0), ("u0", u_held, 0), ("u1", u_held, 1)):
-            tasks += [forward(name, held, b, c) for c in channels]
-        for b in range(BATCH):
-            tasks += [backward([(f"g{b}", "h")], c, store_input(b)) for c in channels]
-        tasks += [backward([("g0", "u0"), ("g1", "u1")], c, store_taps) for c in channels]
-    interleave(tasks, 5)
+    def store_taps(results, channels):
+        for q in range(2):
+            for i, coded in enumerate(encode(*columns(results[q]))):
+                taps_grad[channels[0] // 2, pl.ds(2 * q + i, rows, stride=4), :] = coded
+
+    def forwards(names, half):
+        held = {"g0": (g_held, 0), "g1": (g_held, 1), "h": (h_held, 0), "u0": (u_held, 0), "u1": (u_held, 1)}
+        return [forward(name, *held[name], (2 * half, 2 * half + 1)) for name in names]
+
+    def inputs(half):
+        return [backward([(f"g{b}", "h")], (2 * half, 2 * half + 1), store_input(b)) for b in range(BATCH)]
+
+    def taps_of(half):
+        return [backward([("g0", "u0"), ("g1", "u1")], (2 * half, 2 * half + 1), store_taps)]
+
+    later, ready = forwards(("u0", "u1", "g0", "g1", "h"), 1), inputs(0) + taps_of(0)
+    tasks = forwards(("g0", "g1", "h", "u0", "u1"), 0)
+    tasks += [later[0], ready[0], later[1], ready[1], later[2], later[3], ready[2], later[4]]
+    tasks += taps_of(1) + inputs(1)
+    interleave(tasks, 6)
     for d in range(2):
         out_ref[d * group : (d + 1) * group] = jnp.concatenate(
             [in_grad[d].reshape(group, 16, LANES), taps_grad[d].reshape(group, 8, LANES)], axis=1

time: 65.9 us -> 64.6 us (0.980)
  Pallas kernels: 10.9 us -> 9.53 us
    pallas_call x1, Pallas kernels: 7.67 us -> 6.34 us  [shards(): pl.pallas_call(functools.partial(convolve_kernel, group), out_shape=jax.S...]
where the time goes in v5:
time: 64.6 us; the launch traced here: 64.4 us
  blocking collectives  54.1 us (84%)
  Pallas kernels  9.53 us (15%)
  between operations  0.71 us (1%)
    all_to_all x1, blocking collectives, shards(): lax.all_to_all(packed, ('dp', 'ctx'), split_axis=0, concat_axis=0, tiled=...  33.3 us
    all_to_all x1, blocking collectives, shards(): lax.all_to_all(results, ('dp', 'ctx'), split_axis=0, concat_axis=0, tiled...  20.8 us
    pallas_call x1, Pallas kernels, shards(): pl.pallas_call(functools.partial(convolve_kernel, group), out_shape=jax.S...  6.34 us
    pallas_call x1, Pallas kernels, shards(): pl.pallas_call(functools.partial(pack_kernel, peers), out_shape=jax.Shape...  1.75 us
    pallas_call x1, Pallas kernels, shards(): pl.pallas_call(functools.partial(unpack_kernel, peers), out_shape=(jax.Sh...  1.45 us

profile of v5, /device:TPU:1, one launch (start us, length us, event | category | flops | bytes accessed | tf_op | source)
XLA Modules:
  0.0 64.4 jit_solution(15304520408527073005)
XLA Ops:
  0.6 1.8 %pack.1 = bf16[128,40,128]{2,1,0:T(8,128)(2,1)S(1)} custom-call(bf16[512,512]{1,0:T(8,128)(2,1)} %bitcast.3, bf16[512,512]{1,0:T(8,128)(2,1)} %bitcast.4, bf16[512,512]{1,0:T(8,128)(2,1)} %h_ref.1), custom_call_target="tpu_custom_call" | custom-call | tf_op jit(solution)/shard_map/pack/pallas_call | solution.py:269
  2.4 0.0 copy-start
  2.4 0.0 copy-start.1
  2.4 0.0 copy-start.2
  2.4 0.0 copy-start.3
  2.4 0.0 copy-start.4
  2.5 33.3 %all_to_all.10.in_ref = bf16[128,40,128]{2,1,0:T(8,128)(2,1)S(1)} all-to-all(bf16[128,40,128]{2,1,0:T(8,128)(2,1)S(1)} %pack.1), channel_id=1, replica_groups=mesh['dp'=2,'ctx'=64] {'dp','ctx'}, dimensions={0} | all-to-all | bytes 2621440 | tf_op jit(solution)/shard_map/all_to_all | solution.py:283
  35.8 0.0 copy-done
  35.8 0.0 copy-done.1
  35.8 0.0 copy-done.2
  35.8 0.0 copy-done.3
  35.8 0.0 copy-done.4
  35.8 6.3 %convolve.1 = bf16[128,24,128]{2,1,0:T(8,128)(2,1)S(1)} custom-call(bf16[128,40,128]{2,1,0:T(8,128)(2,1)S(1)} %all_to_all.10.in_ref, bf16[512,256]{1,0:T(8,128)(2,1)S(1)} %copy-done.4, bf16[256,768]{1,0:T(8,128)(2,1)S(1)} %copy-done.2, bf16[768,256]{1,0:T(8,128)(2,1)S(1)} %copy-done.1, bf16[768,256]{1,0:T(8,128)(2,1)S(1)} %copy-done, f32[256,256]{1,0:T(8,128)S(1)} %copy-done.3), custom_call_target="tpu_custom_call" | custom-call | tf_op jit(solution)/shard_map/convolve/pallas_call | solution.py:284
  42.1 20.8 %all_to_all.11.in_ref = bf16[128,24,128]{2,1,0:T(8,128)(2,1)S(1)} all-to-all(bf16[128,24,128]{2,1,0:T(8,128)(2,1)S(1)} %convolve.1), channel_id=1, replica_groups=mesh['dp'=2,'ctx'=64] {'dp','ctx'}, dimensions={0} | all-to-all | bytes 1572864 | tf_op jit(solution)/shard_map/all_to_all | solution.py:297
  63.0 1.4 %unpack.1 = (bf16[512,512]{1,0:T(8,128)(2,1)}, f32[512,256]{1,0:T(8,128)}) custom-call(bf16[128,24,128]{2,1,0:T(8,128)(2,1)S(1)} %all_to_all.11.in_ref), custom_call_target="tpu_custom_call" | custom-call | tf_op jit(solution)/shard_map/unpack/pallas_call | solution.py:298
Async XLA Ops:
  2.4 33.4 %copy-start = (bf16[768,256]{1,0:T(8,128)(2,1)S(1)}, bf16[768,256]{1,0:T(8,128)(2,1)}, u32[]{:S(2)}) copy-start(bf16[768,256]{1,0:T(8,128)(2,1)} %constant.13.clone.back_ref) | copy-start | bytes 1179652
  2.4 33.4 %copy-start.1 = (bf16[768,256]{1,0:T(8,128)(2,1)S(1)}, bf16[768,256]{1,0:T(8,128)(2,1)}, u32[]{:S(2)}) copy-start(bf16[768,256]{1,0:T(8,128)(2,1)} %constant.12.clone.forth_ref) | copy-start | bytes 1179652
  2.4 33.4 %copy-start.2 = (bf16[256,768]{1,0:T(8,128)(2,1)S(1)}, bf16[256,768]{1,0:T(8,128)(2,1)}, u32[]{:S(2)}) copy-start(bf16[256,768]{1,0:T(8,128)(2,1)} %constant.11.clone.last_ref) | copy-start | bytes 1179652
  2.4 33.3 %copy-start.3 = (f32[256,256]{1,0:T(8,128)S(1)}, f32[256,256]{1,0:T(8,128)}, u32[]{:S(2)}) copy-start(f32[256,256]{1,0:T(8,128)} %constant.14.clone.turn_ref) | copy-start | bytes 786436
  2.4 33.3 %copy-start.4 = (bf16[512,256]{1,0:T(8,128)(2,1)S(1)}, bf16[512,256]{1,0:T(8,128)(2,1)}, u32[]{:S(2)}) copy-start(bf16[512,256]{1,0:T(8,128)(2,1)} %constant.10.clone.first_ref) | copy-start | bytes 786436

commit v6 on v5

--- a/solution.py
+++ b/solution.py
@@ -121,9 +121,9 @@
     share = taps_landed.shape[0]
     own = pl.multiple_of(lax.axis_index("dp") * share, share)
     arrivals = (
+        (pltpu.make_async_copy(h_ref.at[pl.ds(own, share), :], taps_landed, sems.at[2]), taps_landed, 32),
         (pltpu.make_async_copy(u_ref, landed.at[0], sems.at[0]), landed.at[0], 0),
         (pltpu.make_async_copy(g_ref, landed.at[1], sems.at[1]), landed.at[1], 16),
-        (pltpu.make_async_copy(h_ref.at[pl.ds(own, share), :], taps_landed, sems.at[2]), taps_landed, 32),
     )
     for copy, _, _ in arrivals:
         copy.start()
@@ -143,15 +143,17 @@
     leaving = []
     for q in range(blocks):
         rows = slice(q * LANES, (q + 1) * LANES)
+        words = [held[pl.ds(16 + 2 * q + c, peers, stride=24), :] for c in range(2)]
+        for c, piece in enumerate(decode(*words)):
+            filter_block[rows, c * peers : (c + 1) * peers] = piece.T
+        leaving.append(pltpu.make_async_copy(filter_block.at[rows], filter_ref.at[rows], sems.at[q]))
+        leaving[-1].start()
+    for q in range(blocks):
+        rows = slice(q * LANES, (q + 1) * LANES)
         for c in range(OWN):
             piece = held[pl.ds(OWN * q + c, peers, stride=24), :]
             input_block[rows, c * peers : (c + 1) * peers] = piece.T.astype(BF16)
-        leaving.append(pltpu.make_async_copy(input_block.at[rows], input_ref.at[rows], sems.at[2 * q]))
-        leaving[-1].start()
-        words = [held[pl.ds(16 + 2 * q + c, peers, stride=24), :] for c in range(2)]
-        for c, piece in enumerate(decode(*words)):
-            filter_block[rows, c * peers : (c + 1) * peers] = piece.T
-        leaving.append(pltpu.make_async_copy(filter_block.at[rows], filter_ref.at[rows], sems.at[2 * q + 1]))
+        leaving.append(pltpu.make_async_copy(input_block.at[rows], input_ref.at[rows], sems.at[blocks + q]))
         leaving[-1].start()
     for copy in leaving:
         copy.wait()
@@ -183,14 +185,15 @@
             both.append(dot(first_ref[2 * rows * q : 2 * rows * (q + 1), :], jnp.concatenate([values, values], axis=0)))
         yield
         sums = (both[0] + both[1], both[0] - both[1])
+        turned = []
         for i, c in enumerate(channels):
-            turned = []
             for m in range(2):
                 turn_cos, turn_sin = turns(m)
                 real, imag = columns(sums[m][0:rows])[i], columns(sums[m][rows : 2 * rows])[i]
                 turned.append(jnp.concatenate([real * turn_cos + imag * turn_sin, imag * turn_cos - real * turn_sin], axis=1))
-            spectra[name, c] = dot(stack(jnp.concatenate(turned, axis=0), 1), forth_ref[...])
-            yield
+        done = dot(stack(jnp.concatenate(turned, axis=0), 1), forth_ref[...])
+        for i, c in enumerate(channels):
+            spectra[name, c] = done[2 * rows * i : 2 * rows * (i + 1)]
         yield
 
     def correlate(left, right, c):
@@ -250,7 +253,7 @@
     tasks = forwards(("g0", "g1", "h", "u0", "u1"), 0)
     tasks += [later[0], ready[0], later[1], ready[1], later[2], later[3], ready[2], later[4]]
     tasks += taps_of(1) + inputs(1)
-    interleave(tasks, 6)
+    interleave(tasks, 5)
     for d in range(2):
         out_ref[d * group : (d + 1) * group] = jnp.concatenate(
             [in_grad[d].reshape(group, 16, LANES), taps_grad[d].reshape(group, 8, LANES)], axis=1

time: 64.6 us -> 64.3 us (level)
  no operation moved by 1% of the time
where the time goes in v6:
time: 64.3 us; the launch traced here: 64.2 us
  blocking collectives  54.2 us (84%)
  Pallas kernels  9.28 us (14%)
  between operations  0.71 us (1%)
    all_to_all x1, blocking collectives, shards(): lax.all_to_all(packed, ('dp', 'ctx'), split_axis=0, concat_axis=0, tiled=...  33.3 us
    all_to_all x1, blocking collectives, shards(): lax.all_to_all(results, ('dp', 'ctx'), split_axis=0, concat_axis=0, tiled...  20.8 us
    pallas_call x1, Pallas kernels, shards(): pl.pallas_call(functools.partial(convolve_kernel, group), out_shape=jax.S...  6.15 us
    pallas_call x1, Pallas kernels, shards(): pl.pallas_call(functools.partial(pack_kernel, peers), out_shape=jax.Shape...  1.7 us
    pallas_call x1, Pallas kernels, shards(): pl.pallas_call(functools.partial(unpack_kernel, peers), out_shape=(jax.Sh...  1.42 us

profile of v6, /device:TPU:1, one launch (start us, length us, event | category | flops | bytes accessed | tf_op | source)
XLA Modules:
  0.0 64.2 jit_solution(10404447177191498074)
XLA Ops:
  0.6 1.7 %pack.1 = bf16[128,40,128]{2,1,0:T(8,128)(2,1)S(1)} custom-call(bf16[512,512]{1,0:T(8,128)(2,1)} %bitcast.3, bf16[512,512]{1,0:T(8,128)(2,1)} %bitcast.4, bf16[512,512]{1,0:T(8,128)(2,1)} %h_ref.1), custom_call_target="tpu_custom_call" | custom-call | tf_op jit(solution)/shard_map/pack/pallas_call | solution.py:272
  2.3 0.0 copy-start
  2.4 0.0 copy-start.1
  2.4 0.0 copy-start.2
  2.4 0.0 copy-start.3
  2.4 0.0 copy-start.4
  2.4 33.3 %all_to_all.10.in_ref = bf16[128,40,128]{2,1,0:T(8,128)(2,1)S(1)} all-to-all(bf16[128,40,128]{2,1,0:T(8,128)(2,1)S(1)} %pack.1), channel_id=1, replica_groups=mesh['dp'=2,'ctx'=64] {'dp','ctx'}, dimensions={0} | all-to-all | bytes 2621440 | tf_op jit(solution)/shard_map/all_to_all | solution.py:286
  35.7 0.0 copy-done
  35.7 0.0 copy-done.1
  35.7 0.0 copy-done.2
  35.7 0.0 copy-done.3
  35.7 0.0 copy-done.4
  35.7 6.1 %convolve.1 = bf16[128,24,128]{2,1,0:T(8,128)(2,1)S(1)} custom-call(bf16[128,40,128]{2,1,0:T(8,128)(2,1)S(1)} %all_to_all.10.in_ref, bf16[512,256]{1,0:T(8,128)(2,1)S(1)} %copy-done.4, bf16[256,768]{1,0:T(8,128)(2,1)S(1)} %copy-done.2, bf16[768,256]{1,0:T(8,128)(2,1)S(1)} %copy-done.1, bf16[768,256]{1,0:T(8,128)(2,1)S(1)} %copy-done, f32[256,256]{1,0:T(8,128)S(1)} %copy-done.3), custom_call_target="tpu_custom_call" | custom-call | tf_op jit(solution)/shard_map/convolve/pallas_call | solution.py:287
  41.9 20.8 %all_to_all.11.in_ref = bf16[128,24,128]{2,1,0:T(8,128)(2,1)S(1)} all-to-all(bf16[128,24,128]{2,1,0:T(8,128)(2,1)S(1)} %convolve.1), channel_id=1, replica_groups=mesh['dp'=2,'ctx'=64] {'dp','ctx'}, dimensions={0} | all-to-all | bytes 1572864 | tf_op jit(solution)/shard_map/all_to_all | solution.py:300
  62.7 1.4 %unpack.1 = (bf16[512,512]{1,0:T(8,128)(2,1)}, f32[512,256]{1,0:T(8,128)}) custom-call(bf16[128,24,128]{2,1,0:T(8,128)(2,1)S(1)} %all_to_all.11.in_ref), custom_call_target="tpu_custom_call" | custom-call | tf_op jit(solution)/shard_map/unpack/pallas_call | solution.py:301
Async XLA Ops:
  2.3 33.4 %copy-start = (bf16[768,256]{1,0:T(8,128)(2,1)S(1)}, bf16[768,256]{1,0:T(8,128)(2,1)}, u32[]{:S(2)}) copy-start(bf16[768,256]{1,0:T(8,128)(2,1)} %constant.13.clone.back_ref) | copy-start | bytes 1179652
  2.4 33.4 %copy-start.1 = (bf16[768,256]{1,0:T(8,128)(2,1)S(1)}, bf16[768,256]{1,0:T(8,128)(2,1)}, u32[]{:S(2)}) copy-start(bf16[768,256]{1,0:T(8,128)(2,1)} %constant.12.clone.forth_ref) | copy-start | bytes 1179652
  2.4 33.4 %copy-start.2 = (bf16[256,768]{1,0:T(8,128)(2,1)S(1)}, bf16[256,768]{1,0:T(8,128)(2,1)}, u32[]{:S(2)}) copy-start(bf16[256,768]{1,0:T(8,128)(2,1)} %constant.11.clone.last_ref) | copy-start | bytes 1179652
  2.4 33.3 %copy-start.3 = (f32[256,256]{1,0:T(8,128)S(1)}, f32[256,256]{1,0:T(8,128)}, u32[]{:S(2)}) copy-start(f32[256,256]{1,0:T(8,128)} %constant.14.clone.turn_ref) | copy-start | bytes 786436
  2.4 33.3 %copy-start.4 = (bf16[512,256]{1,0:T(8,128)(2,1)S(1)}, bf16[512,256]{1,0:T(8,128)(2,1)}, u32[]{:S(2)}) copy-start(bf16[512,256]{1,0:T(8,128)(2,1)} %constant.10.clone.first_ref) | copy-start | bytes 786436

commit v7 on v6

--- a/solution.py
+++ b/solution.py
@@ -134,12 +134,12 @@
             for c in range(OWN):
                 row = first_row + OWN * q + c
                 held[pl.ds(row, peers, stride=40), :] = flipped[c * peers : (c + 1) * peers, :]
-    out_ref[...] = held[...].reshape(peers, 40, LANES).astype(BF16)
+    out_ref[...] = held[0 : peers * 40, :].reshape(peers, 40, LANES).astype(BF16)
 
 
 def unpack_kernel(peers, in_ref, input_ref, filter_ref, held, input_block, filter_block, sems):
     blocks = input_ref.shape[0] // LANES
-    held[...] = in_ref[...].astype(F32).reshape(peers * 24, LANES)
+    held[0 : peers * 24, :] = in_ref[...].astype(F32).reshape(peers * 24, LANES)
     leaving = []
     for q in range(blocks):
         rows = slice(q * LANES, (q + 1) * LANES)
@@ -163,10 +163,10 @@
     rows = 2 * group
     for b in range(BATCH):
         got = in_ref[b * group : (b + 1) * group].astype(F32)
-        u_held[b] = got[:, 0:16].reshape(group * 16, LANES)
-        g_held[b] = got[:, 16:32].reshape(group * 16, LANES)
+        u_held[b, 0 : group * 16, :] = got[:, 0:16].reshape(group * 16, LANES)
+        g_held[b, 0 : group * 16, :] = got[:, 16:32].reshape(group * 16, LANES)
     taps = [in_ref[b * group : (b + 1) * group].astype(F32)[:, 32:40] for b in range(BATCH)]
-    h_held[0] = jnp.concatenate(taps, axis=1).reshape(group * 16, LANES)
+    h_held[0, 0 : group * 16, :] = jnp.concatenate(taps, axis=1).reshape(group * 16, LANES)
 
     def columns(value):
         return value[:, :LANES], value[:, LANES:]
@@ -256,7 +256,7 @@
     interleave(tasks, 5)
     for d in range(2):
         out_ref[d * group : (d + 1) * group] = jnp.concatenate(
-            [in_grad[d].reshape(group, 16, LANES), taps_grad[d].reshape(group, 8, LANES)], axis=1
+            [in_grad[d, 0 : group * 16, :].reshape(group, 16, LANES), taps_grad[d, 0 : group * 8, :].reshape(group, 8, LANES)], axis=1
         ).astype(BF16)
 
 
@@ -277,7 +277,7 @@
         scratch_shapes=[
             pltpu.VMEM((2, local_len, chan_count), BF16),
             pltpu.VMEM((local_len // 2, chan_count), BF16),
-            pltpu.VMEM((peers * 40, LANES), F32),
+            pltpu.VMEM(((peers + 1) * 40, LANES), F32),
             pltpu.SemaphoreType.DMA((3,)),
         ],
         compiler_params=params,
@@ -288,11 +288,11 @@
         functools.partial(convolve_kernel, group),
         out_shape=jax.ShapeDtypeStruct((peers, 24, LANES), BF16),
         scratch_shapes=[
-            pltpu.VMEM((BATCH, group * 16, LANES), F32),
-            pltpu.VMEM((BATCH, group * 16, LANES), F32),
-            pltpu.VMEM((1, group * 16, LANES), F32),
-            pltpu.VMEM((BATCH, group * 16, LANES), F32),
-            pltpu.VMEM((BATCH, group * 8, LANES), F32),
+            pltpu.VMEM((BATCH, group * 16 + 8, LANES), F32),
+            pltpu.VMEM((BATCH, group * 16 + 8, LANES), F32),
+            pltpu.VMEM((1, group * 16 + 8, LANES), F32),
+            pltpu.VMEM((BATCH, group * 16 + 8, LANES), F32),
+            pltpu.VMEM((BATCH, group * 8 + 8, LANES), F32),
         ],
         compiler_params=params,
         name="convolve",
@@ -307,7 +307,7 @@
         in_specs=[local],
         out_specs=(far, far),
         scratch_shapes=[
-            pltpu.VMEM((peers * 24, LANES), F32),
+            pltpu.VMEM(((peers + 1) * 24, LANES), F32),
             pltpu.VMEM((local_len, chan_count), BF16),
             pltpu.VMEM((local_len, chan_count // 2), F32),
             pltpu.SemaphoreType.DMA((2 * (local_len // LANES),)),

time: 64.3 us -> 64.3 us (level)
  no operation moved by 1% of the time
where the time goes in v7:
time: 64.3 us; the launch traced here: 64.2 us
  blocking collectives  54.2 us (84%)
  Pallas kernels  9.27 us (14%)
  between operations  0.71 us (1%)
    all_to_all x1, blocking collectives, shards(): lax.all_to_all(packed, ('dp', 'ctx'), split_axis=0, concat_axis=0, tiled=...  33.3 us
    all_to_all x1, blocking collectives, shards(): lax.all_to_all(results, ('dp', 'ctx'), split_axis=0, concat_axis=0, tiled...  20.8 us
    pallas_call x1, Pallas kernels, shards(): pl.pallas_call(functools.partial(convolve_kernel, group), out_shape=jax.S...  6.14 us
    pallas_call x1, Pallas kernels, shards(): pl.pallas_call(functools.partial(pack_kernel, peers), out_shape=jax.Shape...  1.7 us
    pallas_call x1, Pallas kernels, shards(): pl.pallas_call(functools.partial(unpack_kernel, peers), out_shape=(jax.Sh...  1.42 us

profile of v7, /device:TPU:1, one launch (start us, length us, event | category | flops | bytes accessed | tf_op | source)
XLA Modules:
  0.0 64.2 jit_solution(13936840018012342494)
XLA Ops:
  0.6 1.7 %pack.1 = bf16[128,40,128]{2,1,0:T(8,128)(2,1)S(1)} custom-call(bf16[512,512]{1,0:T(8,128)(2,1)} %bitcast.3, bf16[512,512]{1,0:T(8,128)(2,1)} %bitcast.4, bf16[512,512]{1,0:T(8,128)(2,1)} %h_ref.1), custom_call_target="tpu_custom_call" | custom-call | tf_op jit(solution)/shard_map/pack/pallas_call | solution.py:272
  2.3 0.0 copy-start
  2.4 0.0 copy-start.1
  2.4 0.0 copy-start.2
  2.4 0.0 copy-start.3
  2.4 0.0 copy-start.4
  2.4 33.3 %all_to_all.10.in_ref = bf16[128,40,128]{2,1,0:T(8,128)(2,1)S(1)} all-to-all(bf16[128,40,128]{2,1,0:T(8,128)(2,1)S(1)} %pack.1), channel_id=1, replica_groups=mesh['dp'=2,'ctx'=64] {'dp','ctx'}, dimensions={0} | all-to-all | bytes 2621440 | tf_op jit(solution)/shard_map/all_to_all | solution.py:286
  35.7 0.0 copy-done
  35.7 0.0 copy-done.1
  35.7 0.0 copy-done.2
  35.7 0.0 copy-done.3
  35.7 0.0 copy-done.4
  35.7 6.1 %convolve.1 = bf16[128,24,128]{2,1,0:T(8,128)(2,1)S(1)} custom-call(bf16[128,40,128]{2,1,0:T(8,128)(2,1)S(1)} %all_to_all.10.in_ref, bf16[512,256]{1,0:T(8,128)(2,1)S(1)} %copy-done.4, bf16[256,768]{1,0:T(8,128)(2,1)S(1)} %copy-done.2, bf16[768,256]{1,0:T(8,128)(2,1)S(1)} %copy-done.1, bf16[768,256]{1,0:T(8,128)(2,1)S(1)} %copy-done, f32[256,256]{1,0:T(8,128)S(1)} %copy-done.3), custom_call_target="tpu_custom_call" | custom-call | tf_op jit(solution)/shard_map/convolve/pallas_call | solution.py:287
  41.9 20.8 %all_to_all.11.in_ref = bf16[128,24,128]{2,1,0:T(8,128)(2,1)S(1)} all-to-all(bf16[128,24,128]{2,1,0:T(8,128)(2,1)S(1)} %convolve.1), channel_id=1, replica_groups=mesh['dp'=2,'ctx'=64] {'dp','ctx'}, dimensions={0} | all-to-all | bytes 1572864 | tf_op jit(solution)/shard_map/all_to_all | solution.py:300
  62.7 1.4 %unpack.1 = (bf16[512,512]{1,0:T(8,128)(2,1)}, f32[512,256]{1,0:T(8,128)}) custom-call(bf16[128,24,128]{2,1,0:T(8,128)(2,1)S(1)} %all_to_all.11.in_ref), custom_call_target="tpu_custom_call" | custom-call | tf_op jit(solution)/shard_map/unpack/pallas_call | solution.py:301
Async XLA Ops:
  2.3 33.4 %copy-start = (bf16[768,256]{1,0:T(8,128)(2,1)S(1)}, bf16[768,256]{1,0:T(8,128)(2,1)}, u32[]{:S(2)}) copy-start(bf16[768,256]{1,0:T(8,128)(2,1)} %constant.13.clone.back_ref) | copy-start | bytes 1179652
  2.4 33.4 %copy-start.1 = (bf16[768,256]{1,0:T(8,128)(2,1)S(1)}, bf16[768,256]{1,0:T(8,128)(2,1)}, u32[]{:S(2)}) copy-start(bf16[768,256]{1,0:T(8,128)(2,1)} %constant.12.clone.forth_ref) | copy-start | bytes 1179652
  2.4 33.4 %copy-start.2 = (bf16[256,768]{1,0:T(8,128)(2,1)S(1)}, bf16[256,768]{1,0:T(8,128)(2,1)}, u32[]{:S(2)}) copy-start(bf16[256,768]{1,0:T(8,128)(2,1)} %constant.11.clone.last_ref) | copy-start | bytes 1179652
  2.4 33.3 %copy-start.3 = (f32[256,256]{1,0:T(8,128)S(1)}, f32[256,256]{1,0:T(8,128)}, u32[]{:S(2)}) copy-start(f32[256,256]{1,0:T(8,128)} %constant.14.clone.turn_ref) | copy-start | bytes 786436
  2.4 33.3 %copy-start.4 = (bf16[512,256]{1,0:T(8,128)(2,1)S(1)}, bf16[512,256]{1,0:T(8,128)(2,1)}, u32[]{:S(2)}) copy-start(bf16[512,256]{1,0:T(8,128)(2,1)} %constant.10.clone.first_ref) | copy-start | bytes 786436

commit v8 on v7

--- a/solution.py
+++ b/solution.py
@@ -249,10 +249,10 @@
     def taps_of(half):
         return [backward([("g0", "u0"), ("g1", "u1")], (2 * half, 2 * half + 1), store_taps)]
 
-    later, ready = forwards(("u0", "u1", "g0", "g1", "h"), 1), inputs(0) + taps_of(0)
-    tasks = forwards(("g0", "g1", "h", "u0", "u1"), 0)
-    tasks += [later[0], ready[0], later[1], ready[1], later[2], later[3], ready[2], later[4]]
-    tasks += taps_of(1) + inputs(1)
+    later, ready = forwards(('h', 'u0', 'u1', 'g0', 'g1'), 1), inputs(0) + taps_of(0)
+    tasks = forwards(('g0', 'g1', 'h', 'u0', 'u1'), 0)
+    tasks += [later[0], ready[0], later[1], ready[1], later[2], ready[2], later[3], later[4]]
+    tasks += inputs(1) + taps_of(1)
     interleave(tasks, 5)
     for d in range(2):
         out_ref[d * group : (d + 1) * group] = jnp.concatenate(

time: 64.3 us -> 64.4 us (level)
  no operation moved by 1% of the time
where the time goes in v8:
time: 64.4 us; the launch traced here: 64.2 us
  blocking collectives  54.2 us (84%)
  Pallas kernels  9.31 us (14%)
  between operations  0.7 us (1%)
    all_to_all x1, blocking collectives, shards(): lax.all_to_all(packed, ('dp', 'ctx'), split_axis=0, concat_axis=0, tiled=...  33.3 us
    all_to_all x1, blocking collectives, shards(): lax.all_to_all(results, ('dp', 'ctx'), split_axis=0, concat_axis=0, tiled...  20.8 us
    pallas_call x1, Pallas kernels, shards(): pl.pallas_call(functools.partial(convolve_kernel, group), out_shape=jax.S...  6.19 us
    pallas_call x1, Pallas kernels, shards(): pl.pallas_call(functools.partial(pack_kernel, peers), out_shape=jax.Shape...  1.7 us
    pallas_call x1, Pallas kernels, shards(): pl.pallas_call(functools.partial(unpack_kernel, peers), out_shape=(jax.Sh...  1.42 us

profile of v8, /device:TPU:1, one launch (start us, length us, event | category | flops | bytes accessed | tf_op | source)
XLA Modules:
  0.0 64.2 jit_solution(16181156811101555802)
XLA Ops:
  0.6 1.7 %pack.1 = bf16[128,40,128]{2,1,0:T(8,128)(2,1)S(1)} custom-call(bf16[512,512]{1,0:T(8,128)(2,1)} %bitcast.3, bf16[512,512]{1,0:T(8,128)(2,1)} %bitcast.4, bf16[512,512]{1,0:T(8,128)(2,1)} %h_ref.1), custom_call_target="tpu_custom_call" | custom-call | tf_op jit(solution)/shard_map/pack/pallas_call | solution.py:272
  2.3 0.0 copy-start
  2.4 0.0 copy-start.1
  2.4 0.0 copy-start.2
  2.4 0.0 copy-start.3
  2.4 0.0 copy-start.4
  2.4 33.3 %all_to_all.10.in_ref = bf16[128,40,128]{2,1,0:T(8,128)(2,1)S(1)} all-to-all(bf16[128,40,128]{2,1,0:T(8,128)(2,1)S(1)} %pack.1), channel_id=1, replica_groups=mesh['dp'=2,'ctx'=64] {'dp','ctx'}, dimensions={0} | all-to-all | bytes 2621440 | tf_op jit(solution)/shard_map/all_to_all | solution.py:286
  35.7 0.0 copy-done
  35.7 0.0 copy-done.1
  35.7 0.0 copy-done.2
  35.7 0.0 copy-done.3
  35.7 0.0 copy-done.4
  35.7 6.2 %convolve.1 = bf16[128,24,128]{2,1,0:T(8,128)(2,1)S(1)} custom-call(bf16[128,40,128]{2,1,0:T(8,128)(2,1)S(1)} %all_to_all.10.in_ref, bf16[512,256]{1,0:T(8,128)(2,1)S(1)} %copy-done.4, bf16[256,768]{1,0:T(8,128)(2,1)S(1)} %copy-done.2, bf16[768,256]{1,0:T(8,128)(2,1)S(1)} %copy-done.1, bf16[768,256]{1,0:T(8,128)(2,1)S(1)} %copy-done, f32[256,256]{1,0:T(8,128)S(1)} %copy-done.3), custom_call_target="tpu_custom_call" | custom-call | tf_op jit(solution)/shard_map/convolve/pallas_call | solution.py:287
  41.9 20.8 %all_to_all.11.in_ref = bf16[128,24,128]{2,1,0:T(8,128)(2,1)S(1)} all-to-all(bf16[128,24,128]{2,1,0:T(8,128)(2,1)S(1)} %convolve.1), channel_id=1, replica_groups=mesh['dp'=2,'ctx'=64] {'dp','ctx'}, dimensions={0} | all-to-all | bytes 1572864 | tf_op jit(solution)/shard_map/all_to_all | solution.py:300
  62.8 1.4 %unpack.1 = (bf16[512,512]{1,0:T(8,128)(2,1)}, f32[512,256]{1,0:T(8,128)}) custom-call(bf16[128,24,128]{2,1,0:T(8,128)(2,1)S(1)} %all_to_all.11.in_ref), custom_call_target="tpu_custom_call" | custom-call | tf_op jit(solution)/shard_map/unpack/pallas_call | solution.py:301
Async XLA Ops:
  2.3 33.4 %copy-start = (bf16[768,256]{1,0:T(8,128)(2,1)S(1)}, bf16[768,256]{1,0:T(8,128)(2,1)}, u32[]{:S(2)}) copy-start(bf16[768,256]{1,0:T(8,128)(2,1)} %constant.13.clone.back_ref) | copy-start | bytes 1179652
  2.4 33.4 %copy-start.1 = (bf16[768,256]{1,0:T(8,128)(2,1)S(1)}, bf16[768,256]{1,0:T(8,128)(2,1)}, u32[]{:S(2)}) copy-start(bf16[768,256]{1,0:T(8,128)(2,1)} %constant.12.clone.forth_ref) | copy-start | bytes 1179652
  2.4 33.4 %copy-start.2 = (bf16[256,768]{1,0:T(8,128)(2,1)S(1)}, bf16[256,768]{1,0:T(8,128)(2,1)}, u32[]{:S(2)}) copy-start(bf16[256,768]{1,0:T(8,128)(2,1)} %constant.11.clone.last_ref) | copy-start | bytes 1179652
  2.4 33.3 %copy-start.3 = (f32[256,256]{1,0:T(8,128)S(1)}, f32[256,256]{1,0:T(8,128)}, u32[]{:S(2)}) copy-start(f32[256,256]{1,0:T(8,128)} %constant.14.clone.turn_ref) | copy-start | bytes 786436
  2.4 33.3 %copy-start.4 = (bf16[512,256]{1,0:T(8,128)(2,1)S(1)}, bf16[512,256]{1,0:T(8,128)(2,1)}, u32[]{:S(2)}) copy-start(bf16[512,256]{1,0:T(8,128)(2,1)} %constant.10.clone.first_ref) | copy-start | bytes 786436

commit v9 on v8

--- a/solution.py
+++ b/solution.py
@@ -161,12 +161,19 @@
 
 def convolve_kernel(group, in_ref, first_ref, last_ref, forth_ref, back_ref, turn_ref, out_ref, u_held, g_held, h_held, in_grad, taps_grad):
     rows = 2 * group
-    for b in range(BATCH):
+    arrived = set()
+
+    def arrive(name):
+        if name in arrived:
+            return
+        arrived.add(name)
+        if name == "h":
+            taps = [in_ref[b * group : (b + 1) * group].astype(F32)[:, 32:40] for b in range(BATCH)]
+            h_held[0, 0 : group * 16, :] = jnp.concatenate(taps, axis=1).reshape(group * 16, LANES)
+            return
+        b, held, row = int(name[1]), u_held if name[0] == "u" else g_held, 0 if name[0] == "u" else 16
         got = in_ref[b * group : (b + 1) * group].astype(F32)
-        u_held[b, 0 : group * 16, :] = got[:, 0:16].reshape(group * 16, LANES)
-        g_held[b, 0 : group * 16, :] = got[:, 16:32].reshape(group * 16, LANES)
-    taps = [in_ref[b * group : (b + 1) * group].astype(F32)[:, 32:40] for b in range(BATCH)]
-    h_held[0, 0 : group * 16, :] = jnp.concatenate(taps, axis=1).reshape(group * 16, LANES)
+        held[b, 0 : group * 16, :] = got[:, row : row + 16].reshape(group * 16, LANES)
 
     def columns(value):
         return value[:, :LANES], value[:, LANES:]
@@ -177,6 +184,7 @@
     spectra = {}
 
     def forward(name, held, b, channels):
+        arrive(name)
         both = []
         for q in range(2):
             values = jnp.concatenate(

time: 64.4 us -> 64.4 us (level)
  no operation moved by 1% of the time
where the time goes in v9:
time: 64.4 us; the launch traced here: 64.2 us
  blocking collectives  54.2 us (84%)
  Pallas kernels  9.32 us (14%)
  between operations  0.7 us (1%)
    all_to_all x1, blocking collectives, shards(): lax.all_to_all(packed, ('dp', 'ctx'), split_axis=0, concat_axis=0, tiled=...  33.3 us
    all_to_all x1, blocking collectives, shards(): lax.all_to_all(results, ('dp', 'ctx'), split_axis=0, concat_axis=0, tiled...  20.8 us
    pallas_call x1, Pallas kernels, shards(): pl.pallas_call(functools.partial(convolve_kernel, group), out_shape=jax.S...  6.2 us
    pallas_call x1, Pallas kernels, shards(): pl.pallas_call(functools.partial(pack_kernel, peers), out_shape=jax.Shape...  1.7 us
    pallas_call x1, Pallas kernels, shards(): pl.pallas_call(functools.partial(unpack_kernel, peers), out_shape=(jax.Sh...  1.42 us

profile of v9, /device:TPU:1, one launch (start us, length us, event | category | flops | bytes accessed | tf_op | source)
XLA Modules:
  0.0 64.2 jit_solution(4496134179223187458)
XLA Ops:
  0.6 1.7 %pack.1 = bf16[128,40,128]{2,1,0:T(8,128)(2,1)S(1)} custom-call(bf16[512,512]{1,0:T(8,128)(2,1)} %bitcast.3, bf16[512,512]{1,0:T(8,128)(2,1)} %bitcast.4, bf16[512,512]{1,0:T(8,128)(2,1)} %h_ref.1), custom_call_target="tpu_custom_call" | custom-call | tf_op jit(solution)/shard_map/pack/pallas_call | solution.py:280
  2.3 0.0 copy-start
  2.4 0.0 copy-start.1
  2.4 0.0 copy-start.2
  2.4 0.0 copy-start.3
  2.4 0.0 copy-start.4
  2.4 33.3 %all_to_all.10.in_ref = bf16[128,40,128]{2,1,0:T(8,128)(2,1)S(1)} all-to-all(bf16[128,40,128]{2,1,0:T(8,128)(2,1)S(1)} %pack.1), channel_id=1, replica_groups=mesh['dp'=2,'ctx'=64] {'dp','ctx'}, dimensions={0} | all-to-all | bytes 2621440 | tf_op jit(solution)/shard_map/all_to_all | solution.py:294
  35.7 0.0 copy-done
  35.7 0.0 copy-done.1
  35.7 0.0 copy-done.2
  35.7 0.0 copy-done.3
  35.7 0.0 copy-done.4
  35.7 6.2 %convolve.1 = bf16[128,24,128]{2,1,0:T(8,128)(2,1)S(1)} custom-call(bf16[128,40,128]{2,1,0:T(8,128)(2,1)S(1)} %all_to_all.10.in_ref, bf16[512,256]{1,0:T(8,128)(2,1)S(1)} %copy-done.4, bf16[256,768]{1,0:T(8,128)(2,1)S(1)} %copy-done.2, bf16[768,256]{1,0:T(8,128)(2,1)S(1)} %copy-done.1, bf16[768,256]{1,0:T(8,128)(2,1)S(1)} %copy-done, f32[256,256]{1,0:T(8,128)S(1)} %copy-done.3), custom_call_target="tpu_custom_call" | custom-call | tf_op jit(solution)/shard_map/convolve/pallas_call | solution.py:295
  41.9 20.8 %all_to_all.11.in_ref = bf16[128,24,128]{2,1,0:T(8,128)(2,1)S(1)} all-to-all(bf16[128,24,128]{2,1,0:T(8,128)(2,1)S(1)} %convolve.1), channel_id=1, replica_groups=mesh['dp'=2,'ctx'=64] {'dp','ctx'}, dimensions={0} | all-to-all | bytes 1572864 | tf_op jit(solution)/shard_map/all_to_all | solution.py:308
  62.8 1.4 %unpack.1 = (bf16[512,512]{1,0:T(8,128)(2,1)}, f32[512,256]{1,0:T(8,128)}) custom-call(bf16[128,24,128]{2,1,0:T(8,128)(2,1)S(1)} %all_to_all.11.in_ref), custom_call_target="tpu_custom_call" | custom-call | tf_op jit(solution)/shard_map/unpack/pallas_call | solution.py:309
Async XLA Ops:
  2.3 33.4 %copy-start = (bf16[768,256]{1,0:T(8,128)(2,1)S(1)}, bf16[768,256]{1,0:T(8,128)(2,1)}, u32[]{:S(2)}) copy-start(bf16[768,256]{1,0:T(8,128)(2,1)} %constant.13.clone.back_ref) | copy-start | bytes 1179652
  2.4 33.4 %copy-start.1 = (bf16[768,256]{1,0:T(8,128)(2,1)S(1)}, bf16[768,256]{1,0:T(8,128)(2,1)}, u32[]{:S(2)}) copy-start(bf16[768,256]{1,0:T(8,128)(2,1)} %constant.12.clone.forth_ref) | copy-start | bytes 1179652
  2.4 33.4 %copy-start.2 = (bf16[256,768]{1,0:T(8,128)(2,1)S(1)}, bf16[256,768]{1,0:T(8,128)(2,1)}, u32[]{:S(2)}) copy-start(bf16[256,768]{1,0:T(8,128)(2,1)} %constant.11.clone.last_ref) | copy-start | bytes 1179652
  2.4 33.3 %copy-start.3 = (f32[256,256]{1,0:T(8,128)S(1)}, f32[256,256]{1,0:T(8,128)}, u32[]{:S(2)}) copy-start(f32[256,256]{1,0:T(8,128)} %constant.14.clone.turn_ref) | copy-start | bytes 786436
  2.4 33.3 %copy-start.4 = (bf16[512,256]{1,0:T(8,128)(2,1)S(1)}, bf16[512,256]{1,0:T(8,128)(2,1)}, u32[]{:S(2)}) copy-start(bf16[512,256]{1,0:T(8,128)(2,1)} %constant.10.clone.first_ref) | copy-start | bytes 786436
